TPU v7x, 128 devices: a whole 4x4x4 slice. The times are simulated.
128 devices in a mesh: tile: 32 (over z, y, core), dom: 4 (over x).
Axes of the slice: x: 4, y: 4, z: 4, core: 2. Of those that a mesh axis runs over, the one named last changes fastest.
Arguments:
- grid_latent: bfloat16 [262144, 512], P(('tile', 'dom')), may hold values from -6 to 6
- mesh_latent: bfloat16 [131072, 512], P(('tile', 'dom')), may hold values from -6 to 6
- g2m_send: int32 [128, 128], P(('tile', 'dom')), may hold values from 0 to 31
- g2m_src: int32 [128, 224], P(('tile', 'dom')), may hold values from 0 to 159, as said below
- g2m_dst: int32 [128, 224], P(('tile', 'dom')), may hold values from 0 to 15, as said below
- g2m_weight: bfloat16 [28672, 64, 64], P(('tile', 'dom')), may hold values from -0.1875 to 0.1875
- halo_send: int32 [128, 8], P(('tile', 'dom')), may hold values from 0 to 15
- m2m_src: int32 [128, 112], P(('tile', 'dom')), may hold values from 0 to 31, as said below
- m2m_dst: int32 [128, 112], P(('tile', 'dom')), may hold values from 0 to 15, as said below
- m2m_weight: bfloat16 [2, 14336, 64, 64], P(None, ('tile', 'dom')), may hold values from -0.25 to 0.25
- enc_msg_in: bfloat16 [512, 512], replicated, may hold values from -0.25 to 0.25
- enc_msg_out: bfloat16 [512, 512], replicated, may hold values from -0.25 to 0.25
- enc_upd_in: bfloat16 [1024, 512], replicated, may hold values from -0.1875 to 0.1875
- enc_upd_out: bfloat16 [512, 512], replicated, may hold values from -0.25 to 0.25
- enc_gain: float32 [512], replicated, may hold values from 0.1 to 1.9
- proc_msg_in: bfloat16 [2, 512, 512], replicated, may hold values from -0.25 to 0.25
- proc_msg_out: bfloat16 [2, 512, 512], replicated, may hold values from -0.25 to 0.25
- proc_upd_in: bfloat16 [2, 1024, 512], replicated, may hold values from -0.1875 to 0.1875
- proc_upd_out: bfloat16 [2, 512, 512], replicated, may hold values from -0.25 to 0.25
- proc_gain: float32 [2, 512], replicated, may hold values from 0.1 to 1.9
Outputs:
- mesh_out: bfloat16 [131072, 512], P(('tile', 'dom'))
Inputs may be any that keep to these rules, and one draw needn't show every extreme that they name: `g2m_src`: in each row every number from 0 to 159 appears at least once; below 32 it names the device's own grid block, 32 + p the block sent by device p. `g2m_dst`: in each row every mesh block is named by 14 tiles or one more. `m2m_src`: in each row every number from 0 to 31 appears at least once; below 16 it names an own block, then the lower neighbour's rim blocks, then the upper's. `m2m_dst`: in each row every mesh block is named by 7 tiles or one more.
All inputs are finite; a program needn't handle non-finite values.
Results may differ from a plain program's by a relative error of at most 0.018.
Values may be sent and summed in bfloat16 or wider, within the bound.
A program may use at most 128 MiB of HBM per device.

v0:
```python
import jax
import jax.numpy as jnp
from jax import lax
from jax.sharding import PartitionSpec as P


def extended(block, sides, width):
    for axis, dim in sides:
        count = lax.axis_size(axis)
        forward = [(i, i + 1) for i in range(count - 1)]
        forward.append((count - 1, 0))
        backward = [(target, source) for source, target in forward]
        low = lax.ppermute(
            lax.slice_in_dim(block, block.shape[dim] - width, None, axis=dim), axis, forward
        )
        high = lax.ppermute(lax.slice_in_dim(block, 0, width, axis=dim), axis, backward)
        block = jnp.concatenate([low, block, high], axis=dim)
    return block


def two_layer(inputs, w_in, w_out):
    hidden = jax.nn.silu(jnp.dot(inputs, w_in, preferred_element_type=jnp.float32)).astype(
        jnp.bfloat16
    )
    return jnp.dot(hidden, w_out, preferred_element_type=jnp.float32).astype(jnp.bfloat16)


def aggregate(source_table, sources, targets, weight, blocks):
    tile_count = targets.shape[0]
    tile_rows = weight.shape[1]
    width = -(-tile_count // blocks)
    matches = (targets[:, None] == jnp.arange(blocks, dtype=jnp.int32)[None, :]).astype(jnp.int32)
    counts = jnp.sum(matches, axis=0)
    starts = jnp.cumsum(counts) - counts
    order = jnp.argsort(targets, stable=True)
    sorted_targets = targets[order]
    position = jnp.arange(tile_count, dtype=jnp.int32) - starts[sorted_targets]
    slots = jnp.full((blocks, width), tile_count, jnp.int32).at[sorted_targets, position].set(order)
    padded_weight = jnp.concatenate(
        [weight, jnp.zeros((1, tile_rows, tile_rows), weight.dtype)], axis=0
    )
    padded_sources = jnp.concatenate([sources, jnp.zeros((1,), jnp.int32)], axis=0)
    slot_weight = padded_weight[slots]
    slot_rows = source_table[padded_sources[slots]]
    summed = jnp.einsum(
        "bkij,bkid->bjd", slot_weight, slot_rows, preferred_element_type=jnp.float32
    )
    return summed.astype(jnp.bfloat16)


def update(latent, summed, w_in, w_out, norm_gain):
    features = latent.shape[1]
    pre_sum = jnp.dot(latent, w_in[:features], preferred_element_type=jnp.float32)
    pre_sum = pre_sum + jnp.dot(summed, w_in[features:], preferred_element_type=jnp.float32)
    hidden = jax.nn.silu(pre_sum).astype(jnp.bfloat16)
    output_rows = jnp.dot(hidden, w_out, preferred_element_type=jnp.float32)
    row_mean = jnp.mean(output_rows, axis=1, keepdims=True)
    centred = output_rows - row_mean
    row_var = jnp.mean(centred * centred, axis=1, keepdims=True)
    normed = centred * lax.rsqrt(row_var + 1e-05) * norm_gain
    return (latent.astype(jnp.float32) + normed).astype(jnp.bfloat16)


def on_device(
    grid_latent,
    mesh_latent,
    g2m_send,
    g2m_src,
    g2m_dst,
    g2m_weight,
    halo_send,
    m2m_src,
    m2m_dst,
    m2m_weight,
    enc_msg_in,
    enc_msg_out,
    enc_upd_in,
    enc_upd_out,
    enc_gain,
    proc_msg_in,
    proc_msg_out,
    proc_upd_in,
    proc_upd_out,
    proc_gain,
):
    features = grid_latent.shape[1]
    tile_rows = g2m_weight.shape[1]
    mesh_count = mesh_latent.shape[0] // tile_rows
    grid_msg = two_layer(grid_latent, enc_msg_in, enc_msg_out).reshape(-1, tile_rows, features)
    outgoing = grid_msg[g2m_send[0]]
    incoming = lax.all_to_all(outgoing, ("tile", "dom"), split_axis=0, concat_axis=0, tiled=True)
    source_table = jnp.concatenate([grid_msg, incoming], axis=0)
    summed = aggregate(source_table, g2m_src[0], g2m_dst[0], g2m_weight, mesh_count)
    mesh_state = update(
        mesh_latent, summed.reshape(-1, features), enc_upd_in, enc_upd_out, enc_gain
    )
    rim_count = halo_send.shape[1]
    for layer_index in range(proc_msg_in.shape[0]):
        own_msg = two_layer(
            mesh_state, proc_msg_in[layer_index], proc_msg_out[layer_index]
        ).reshape(-1, tile_rows, features)
        payload = own_msg[halo_send[0]]
        beside_all = extended(payload, (("dom", 0),), rim_count)
        rim_msg = jnp.concatenate([beside_all[:rim_count], beside_all[2 * rim_count :]], axis=0)
        source_table = jnp.concatenate([own_msg, rim_msg], axis=0)
        summed = aggregate(
            source_table, m2m_src[0], m2m_dst[0], m2m_weight[layer_index], mesh_count
        )
        mesh_state = update(
            mesh_state,
            summed.reshape(-1, features),
            proc_upd_in[layer_index],
            proc_upd_out[layer_index],
            proc_gain[layer_index],
        )
    return mesh_state


def solution(mesh):
    placed = (
        P(("tile", "dom"), None),
        P(("tile", "dom"), None),
        P(("tile", "dom"), None),
        P(("tile", "dom"), None),
        P(("tile", "dom"), None),
        P(("tile", "dom"), None, None),
        P(("tile", "dom"), None),
        P(("tile", "dom"), None),
        P(("tile", "dom"), None),
        P(None, ("tile", "dom"), None, None),
        P(),
        P(),
        P(),
        P(),
        P(),
        P(),
        P(),
        P(),
        P(),
        P(),
    )
    return jax.shard_map(
        on_device, mesh=mesh, in_specs=placed, out_specs=P(("tile", "dom"), None), check_vma=False
    )
```

profile of v0, /device:TPU:6, one launch (start us, length us, event | category | flops | bytes accessed | tf_op | source)
XLA Modules:
  0.0 251.6 jit_solution(4138516537220192560)
XLA Ops:
  0.0 0.8 fusion.53
  0.8 0.8 copy-done
  1.6 5.3 %convolution_convert_fusion = bf16[2048,512]{1,0:T(8,128)(2,1)} fusion(bf16[512,512]{1,0:T(8,128)(2,1)} %param.31, bf16[2048,512]{1,0:T(8,128)(2,1)S(1)} %copy-done, bf16[512,512]{1,0:T(8,128)(2,1)} %param.30), kind=kOutput, calls=%fused_computation.17 | convolution fusion | flops 2153775104 | bytes 5242880 | tf_op jit(solution)/shard_map/dot_general | solution.py:25
  6.9 8.1 %gather_fusion.2 = bf16[128,64,512]{2,1,0:T(8,128)(2,1)} fusion(bf16[32,64,512]{2,1,0:T(8,128)(2,1)} %bitcast.284, s32[1024]{0:T(1024)S(1)} %pad_clamp_fusion.5), kind=kCustom, calls=%fused_computation.2 | custom fusion | bytes 16777728 | tf_op jit(solution)/shard_map/gather | solution.py:90
  15.0 11.7 %all-to-all-start = ((bf16[128,64,512]{2,1,0:T(8,128)(2,1)}), bf16[128,64,512]{2,1,0:T(8,128)(2,1)}, u32[]{:S(2)}, u32[]{:S(2)}) async-start(bf16[128,64,512]{2,1,0:T(8,128)(2,1)} %gather_fusion.2), calls=%async_computation | async-start | bytes 16777216 | tf_op jit(solution)/shard_map/all_to_all | solution.py:91
  27.1 3.2 %sort.36 = (s32[224]{0:T(256)}, s32[224]{0:T(256)S(1)}) sort(s32[224]{0:T(256)S(1)} %bitcast.278, s32[224]{0:T(256)S(1)} %iota.25), dimensions={0}, to_apply=%region_0.1 | sort | flops 1792 | bytes 3584 | tf_op jit(solution)/shard_map/jit(argsort)/sort | solution.py:35
  30.3 1.9 gather_fusion
  32.2 0.7 fusion.65
  33.0 4.4 %compare_select_fusion.6 = (s32[224,1]{0,1:T(1,128)S(1)}, s32[224,1]{0,1:T(1,128)S(1)}) fusion(s32[]{:T(128)} %bitcast.12, s32[]{:T(128)} %bitcast.13, s32[]{:T(128)} %bitcast.14, s32[]{:T(128)} %bitcast.15, s32[]{:T(128)} %bitcast.16, s32[]{:T(128)} %bitcast.18, s32[]{:T(128)} %bitcast.17, s32[224,1]{0,1:T(1,128)S(1)} %bitcast.305), kind=kLoop, calls=%fused_computation.99 | loop fusion | flops 3360 | bytes 2716 | tf_op jit(solution)/shard_map/gather | solution.py:37
  37.4 5.6 %select_select_fusion = s32[224]{0:T(256)S(1)} fusion(pred[224]{0:T(512)(128)(4,1)S(1)} %get-tuple-element.17, pred[224]{0:T(512)(128)(4,1)S(1)} %get-tuple-element.15, pred[224]{0:T(512)(128)(4,1)S(1)} %get-tuple-element.14, pred[224]{0:T(512)(128)(4,1)S(1)} %get-tuple-element.13, pred[224]{0:T(512)(128)(4,1)S(1)} %get-tuple-element.12, ...), kind=kLoop, calls=%fused_computation.135 | loop fusion | flops 2016 | bytes 3844 | tf_op jit(solution)/shard_map/gather | solution.py:37
  43.0 11.9 %scatter_fusion = s32[16,14]{1,0:T(8,128)S(1)} fusion(s32[16,14]{1,0:T(8,128)S(1)} %broadcast_in_dim.10, s32[224]{0:T(256)S(1)} %bitcast.289, s32[224]{0:T(256)S(1)} %get-tuple-element.7), kind=kCustom, calls=%fused_computation.13 | custom fusion | bytes 4480 | tf_op jit(solution)/shard_map/scatter | solution.py:38
  55.1 1.9 gather_fusion.3
  57.3 5.6 %copy.41 = bf16[224,64,64]{2,1,0:T(8,128)(2,1)} copy(bf16[224,64,64]{0,2,1:T(8,128)(2,1)} %param.25) | data formatting | bytes 3670016 | tf_op args[5]
  62.9 4.9 %concatenate.32 = bf16[225,64,64]{2,1,0:T(8,128)(2,1)} pad(bf16[224,64,64]{2,1,0:T(8,128)(2,1)} %copy.41, bf16[]{:T(256)} %constant.16.clone.1), padding=0_1x0_0x0_0 | pad | bytes 3678210 | tf_op jit(solution)/shard_map/concatenate | solution.py:39
  67.8 5.1 %gather_fusion.1 = bf16[224,64,64]{2,1,0:T(8,128)(2,1)} fusion(bf16[225,64,64]{2,1,0:T(8,128)(2,1)} %concatenate.32, s32[1024]{0:T(1024)S(1)} %pad_clamp_fusion.6), kind=kCustom, calls=%fused_computation.1 | custom fusion | bytes 3670912 | tf_op jit(solution)/shard_map/gather | solution.py:43
  72.8 1.3 copy.40
  74.5 2.5 %sort.37 = (s32[112]{0:T(128)}, s32[112]{0:T(128)S(1)}) sort(s32[112]{0:T(128)S(1)} %bitcast.281, s32[112]{0:T(128)S(1)} %iota.27), dimensions={0}, to_apply=%region_6.7 | sort | flops 784 | bytes 1792 | tf_op jit(solution)/shard_map/jit(argsort)/sort | solution.py:35
  77.1 1.2 gather_fusion.5
  78.3 0.7 fusion.64
  79.0 9.9 %fusion.55 = s32[112]{0:T(128)S(1)} fusion(s32[112]{0:T(128)S(1)} %gather_fusion.5, s32[]{:T(128)} %bitcast.54, s32[]{:T(128)} %bitcast.55, s32[]{:T(128)} %bitcast.56, s32[]{:T(128)} %bitcast.57, s32[]{:T(128)} %bitcast.58, s32[]{:T(128)} %bitcast.60, s32[]{:T(128)} %bitcast.59, s32[]{:T(128)} %bitcast.37, s32[]{:T(128)} %bitcast.39, s32[]{:T(128)} %bitcast.41, ...), kind=kLoop, calls=%fused_computation.145 | loop fusion | flops 5152 | bytes 960 | tf_op jit(solution)/shard_map/concatenate | solution.py:38
  88.9 5.7 %scatter_fusion.1 = s32[16,7]{0,1:T(8,128)S(1)} fusion(s32[16,7]{0,1:T(8,128)S(1)} %broadcast.243, s32[112]{0:T(128)S(1)} %fusion.55, s32[112]{0:T(128)S(1)} %get-tuple-element.8), kind=kCustom, calls=%fused_computation.14 | custom fusion | bytes 2240 | tf_op jit(solution)/shard_map/scatter | solution.py:38
  94.9 1.2 gather_fusion.8
  96.3 2.7 %fusion.62 = (bf16[1,112,64,64]{1,3,2,0:T(8,128)(2,1)}, bf16[1,112,64,64]{1,3,2,0:T(8,128)(2,1)S(1)}) fusion(bf16[2,112,64,64]{1,3,2,0:T(8,128)(2,1)} %param.29), kind=kLoop, calls=%fused_computation.152 | loop fusion | bytes 3670016 | tf_op jit(solution)/shard_map/slice | solution.py:107
  99.0 3.5 %copy.57 = bf16[1,112,64,64]{3,2,1,0:T(8,128)(2,1)} copy(bf16[1,112,64,64]{1,3,2,0:T(8,128)(2,1)S(1)} %get-tuple-element.21) | data formatting | bytes 1835008
  102.5 2.0 concatenate.36
  104.6 2.0 gather_fusion.6
  106.7 3.2 %fusion.46 = f32[1024,512]{1,0:T(8,128)} fusion(bf16[1024,512]{1,0:T(8,128)(2,1)S(1)} %copy-done.9, bf16[1024,512]{1,0:T(8,128)(2,1)} %param.32), kind=kOutput, calls=%fused_computation.67 | convolution fusion | flops 536870912 | bytes 3670016 | tf_op jit(solution)/shard_map/dot_general | solution.py:53
  109.9 19.5 %all-to-all-done = bf16[128,64,512]{2,1,0:T(8,128)(2,1)} async-done(((bf16[128,64,512]{2,1,0:T(8,128)(2,1)}), bf16[128,64,512]{2,1,0:T(8,128)(2,1)}, u32[]{:S(2)}, u32[]{:S(2)}) %all-to-all-start) | async-done | bytes 8388640 | tf_op jit(solution)/shard_map/all_to_all | solution.py:91
  129.4 8.7 %pad_maximum_fusion = bf16[160,64,512]{2,1,0:T(8,128)(2,1)} fusion(bf16[128,64,512]{2,1,0:T(8,128)(2,1)} %all-to-all-done, bf16[32,64,512]{2,1,0:T(8,128)(2,1)S(1)} %bitcast.285), kind=kLoop, calls=%fused_computation.15 | loop fusion | flops 5242880 | bytes 20971520 | tf_op jit(solution)/shard_map/concatenate | solution.py:92
  138.0 13.4 %gather_fusion.4 = bf16[224,64,512]{2,1,0:T(8,128)(2,1)} fusion(bf16[160,64,512]{2,1,0:T(8,128)(2,1)} %pad_maximum_fusion, s32[1024]{0:T(1024)S(1)} %pad_clamp_fusion.4), kind=kCustom, calls=%fused_computation.4 | custom fusion | bytes 29361024 | tf_op jit(solution)/shard_map/gather | solution.py:44
  151.4 9.0 %bitcast_convert_fusion.2 = bf16[16,64,512]{2,1,0:T(8,128)(2,1)S(1)} fusion(bf16[16,14,64,64]{3,2,1,0:T(8,128)(2,1)} %bitcast.288, bf16[16,14,64,512]{3,2,1,0:T(8,128)(2,1)} %bitcast.283), kind=kOutput, calls=%fused_computation.22 | convolution fusion | flops 940048384 | bytes 17563648 | tf_op jit(solution)/shard_map/bkij,bkid->bjd/dot_general | solution.py:45
  160.4 3.4 %fusion.66 = (f32[1024]{0:T(1024)S(1)}, f32[1024,512]{0,1:T(8,128)S(1)}) fusion(bf16[512,512]{1,0:T(8,128)(2,1)} %param.33, f32[1024,512]{1,0:T(8,128)} %fusion.46, bf16[1024,512]{1,0:T(8,128)(2,1)S(1)} %bitcast.300, bf16[1024,512]{1,0:T(8,128)(2,1)} %param.32), kind=kOutput, calls=%fused_computation.156 | convolution fusion | flops 1077410816 | bytes 6295552 | tf_op jit(solution)/shard_map/dot_general | solution.py:56
  163.8 0.3 multiply_reduce_fusion.2
  164.1 1.0 copy-done.8
  165.1 0.6 copy-done.10
  165.8 2.0 add_convert_fusion.2
  167.8 3.0 %convolution_convert_fusion.2 = bf16[1024,512]{1,0:T(8,128)(2,1)S(1)} fusion(bf16[1024,512]{0,1:T(8,128)(2,1)S(1)} %add_convert_fusion.2, bf16[2,512,512]{2,1,0:T(8,128)(2,1)} %param.36, bf16[2,512,512]{2,1,0:T(8,128)(2,1)} %param.35), kind=kOutput, calls=%fused_computation.35 | convolution fusion | flops 1076887552 | bytes 3145728 | tf_op jit(solution)/shard_map/dot_general | solution.py:25
  170.9 0.6 gather_fusion.7
  171.5 0.8 collective-permute-start
  172.2 1.3 collective-permute-start.1
  173.6 3.2 %fusion.28 = f32[1024,512]{1,0:T(8,128)} fusion(bf16[1024,512]{0,1:T(8,128)(2,1)S(1)} %add_convert_fusion.2, bf16[2,1024,512]{2,1,0:T(8,128)(2,1)} %param.37), kind=kOutput, calls=%fused_computation.54 | convolution fusion | flops 536870912 | bytes 3670016 | tf_op jit(solution)/shard_map/dot_general | solution.py:53
  176.8 8.3 %collective-permute-done = bf16[8,64,512]{2,1,0:T(8,128)(2,1)S(1)} collective-permute-done((bf16[8,64,512]{2,1,0:T(8,128)(2,1)S(1)}, bf16[8,64,512]{2,1,0:T(8,128)(2,1)S(1)}, u32[]{:S(2)}, u32[]{:S(2)}) %collective-permute-start) | collective-permute-done | bytes 524320 | tf_op jit(solution)/shard_map/ppermute | solution.py:13
  185.0 2.2 collective-permute-done.1
  187.5 6.5 %gather_fusion.9 = bf16[112,64,512]{2,1,0:T(8,128)(2,1)} fusion(bf16[32,64,512]{2,1,0:T(8,128)(2,1)S(1)} %pad_maximum_fusion.1, s32[1024]{0:T(1024)S(1)} %pad_clamp_fusion), kind=kCustom, calls=%fused_computation.9 | custom fusion | bytes 14680512 | tf_op jit(solution)/shard_map/gather | solution.py:44
  194.0 5.2 %bitcast_convert_fusion.1 = bf16[16,64,512]{2,1,0:T(8,128)(2,1)S(1)} fusion(bf16[16,7,64,64]{3,2,1,0:T(8,128)(2,1)} %bitcast.290, bf16[16,7,64,512]{3,2,1,0:T(8,128)(2,1)} %bitcast.287), kind=kOutput, calls=%fused_computation.21 | convolution fusion | flops 470286336 | bytes 9306112 | tf_op jit(solution)/shard_map/bkij,bkid->bjd/dot_general | solution.py:45
  199.2 4.6 %fusion.69 = (f32[1024]{0:T(1024)S(1)}, f32[1024,512]{0,1:T(8,128)}) fusion(bf16[2,512,512]{2,1,0:T(8,128)(2,1)S(1)} %copy-done.17, f32[1024,512]{1,0:T(8,128)} %fusion.28, bf16[1024,512]{1,0:T(8,128)(2,1)S(1)} %bitcast.294, bf16[2,1024,512]{2,1,0:T(8,128)(2,1)} %param.37), kind=kOutput, calls=%fused_computation.157 | convolution fusion | flops 1077410816 | bytes 6295552 | tf_op jit(solution)/shard_map/dot_general | solution.py:56
  203.9 1.9 multiply_reduce_fusion.1
  205.8 2.0 add_convert_fusion.1
  207.8 2.7 %convolution_convert_fusion.1 = bf16[1024,512]{1,0:T(8,128)(2,1)S(1)} fusion(bf16[1024,512]{0,1:T(8,128)(2,1)S(1)} %add_convert_fusion.1, bf16[2,512,512]{2,1,0:T(8,128)(2,1)} %param.36, bf16[2,512,512]{2,1,0:T(8,128)(2,1)} %param.35), kind=kOutput, calls=%fused_computation.34 | convolution fusion | flops 1076887552 | bytes 3145728 | tf_op jit(solution)/shard_map/dot_general | solution.py:25
  210.6 1.4 gather_fusion.11
  212.0 0.3 collective-permute-start.2
  212.3 1.7 collective-permute-start.3
  214.0 3.7 %copy.58 = bf16[1,112,64,64]{3,2,1,0:T(8,128)(2,1)} copy(bf16[1,112,64,64]{1,3,2,0:T(8,128)(2,1)S(1)} %copy-done.11) | data formatting | bytes 1835008
  217.7 2.0 concatenate.40
  219.8 2.0 gather_fusion.10
  221.8 3.3 %fusion.16 = f32[1024,512]{1,0:T(8,128)} fusion(bf16[1024,512]{0,1:T(8,128)(2,1)S(1)} %add_convert_fusion.1, bf16[2,1024,512]{2,1,0:T(8,128)(2,1)} %param.37), kind=kOutput, calls=%fused_computation.47 | convolution fusion | flops 536870912 | bytes 3670016 | tf_op jit(solution)/shard_map/dot_general | solution.py:53
  225.2 1.5 collective-permute-done.3
  226.8 1.4 pad_maximum_fusion.2
  228.2 6.3 %gather_fusion.12 = bf16[112,64,512]{2,1,0:T(8,128)(2,1)} fusion(bf16[32,64,512]{2,1,0:T(8,128)(2,1)S(1)} %pad_maximum_fusion.2, s32[1024]{0:T(1024)S(1)} %pad_clamp_fusion), kind=kCustom, calls=%fused_computation.12 | custom fusion | bytes 14680512 | tf_op jit(solution)/shard_map/gather | solution.py:44
  234.5 6.1 %bitcast_convert_fusion = bf16[16,64,512]{2,1,0:T(8,128)(2,1)} fusion(bf16[16,7,64,64]{3,2,1,0:T(8,128)(2,1)} %bitcast.291, bf16[16,7,64,512]{3,2,1,0:T(8,128)(2,1)} %bitcast.286), kind=kOutput, calls=%fused_computation.20 | convolution fusion | flops 470286336 | bytes 9306112 | tf_op jit(solution)/shard_map/bkij,bkid->bjd/dot_general | solution.py:45
  240.6 3.7 %fusion.72 = (f32[1024]{0:T(1024)S(1)}, f32[1024,512]{0,1:T(8,128)S(1)}) fusion(bf16[2,512,512]{2,1,0:T(8,128)(2,1)} %param.38, f32[1024,512]{1,0:T(8,128)} %fusion.16, bf16[1024,512]{1,0:T(8,128)(2,1)} %bitcast.295, bf16[2,1024,512]{2,1,0:T(8,128)(2,1)} %param.37), kind=kOutput, calls=%fused_computation.158 | convolution fusion | flops 1077410816 | bytes 6295552 | tf_op jit(solution)/shard_map/dot_general | solution.py:56
  244.3 1.3 copy-done.7
  246.0 3.1 %add_convert_fusion = bf16[1024,512]{0,1:T(8,128)(2,1)} fusion(bf16[1024,512]{0,1:T(8,128)(2,1)S(1)} %add_convert_fusion.1, f32[1024,512]{0,1:T(8,128)} %copy-done.7, f32[512]{0:T(512)S(1)} %bitcast.301, f32[1024]{0:T(1024)S(1)} %add_rsqrt_fusion, f32[1024]{0:T(1024)S(1)} %broadcast_multiply_fusion), kind=kLoop, calls=%fused_computation.23 | loop fusion | flops 3145728 | bytes 4204544 | tf_op jit(solution)/shard_map/convert_element_type | solution.py:61
  249.1 2.3 copy.50
  (86 shorter events, 2.5 us)
Async XLA Ops:
  0.0 1.6 copy-start
  15.0 11.7 %copy-start.2 = (s32[1,224]{1,0:T(1,128)S(1)}, s32[1,224]{1,0:T(1,128)}, u32[]{:S(2)}) copy-start(s32[1,224]{1,0:T(1,128)} %param.24) | copy-start | bytes 2692
  15.0 114.3 %all-to-all-start = ((bf16[128,64,512]{2,1,0:T(8,128)(2,1)}), bf16[128,64,512]{2,1,0:T(8,128)(2,1)}, u32[]{:S(2)}, u32[]{:S(2)}) async-start(bf16[128,64,512]{2,1,0:T(8,128)(2,1)} %gather_fusion.2), calls=%async_computation | async-start | bytes 16777216 | tf_op jit(solution)/shard_map/all_to_all | solution.py:91
  26.7 28.3 %copy-start.16 = (s32[1,224]{1,0:T(1,128)S(1)}, s32[1,224]{1,0:T(1,128)}, u32[]{:S(2)}) copy-start(s32[1,224]{1,0:T(1,128)} %param.23) | copy-start | bytes 2692
  67.8 5.1 %copy-start.9 = (bf16[1024,512]{1,0:T(8,128)(2,1)S(1)}, bf16[1024,512]{1,0:T(8,128)(2,1)}, u32[]{:S(2)}) copy-start(bf16[1024,512]{1,0:T(8,128)(2,1)} %param.21) | copy-start | bytes 3145732
  72.8 1.3 copy-start.3
  72.8 22.0 %copy-start.18 = (s32[1,112]{1,0:T(1,128)S(1)}, s32[1,112]{1,0:T(1,128)}, u32[]{:S(2)}) copy-start(s32[1,112]{1,0:T(1,128)} %param.27) | copy-start | bytes 1348
  104.6 2.1 copy-start.19
  106.6 22.8 %copy-start.4 = (bf16[2048,512]{1,0:T(8,128)(2,1)S(1)}, bf16[2048,512]{1,0:T(8,128)(2,1)}, u32[]{:S(2)}) copy-start(bf16[2048,512]{1,0:T(8,128)(2,1)} %convolution_convert_fusion) | copy-start | bytes 6291460
  163.8 1.4 copy-start.8
  163.8 2.0 copy-start.10
  163.8 2.0 copy-start.15
  167.8 5.8 %copy-start.5 = (bf16[1024,512]{0,1:T(8,128)(2,1)}, bf16[1024,512]{0,1:T(8,128)(2,1)S(1)}, u32[]{:S(2)}) copy-start(bf16[1024,512]{0,1:T(8,128)(2,1)S(1)} %add_convert_fusion.2) | copy-start | bytes 3145732
  167.8 5.8 %copy-start.14 = (f32[2,512]{1,0:T(2,128)S(1)}, f32[2,512]{1,0:T(2,128)}, u32[]{:S(2)}) copy-start(f32[2,512]{1,0:T(2,128)} %param.39) | copy-start | bytes 12292
  171.5 13.6 %collective-permute-start = (bf16[8,64,512]{2,1,0:T(8,128)(2,1)S(1)}, bf16[8,64,512]{2,1,0:T(8,128)(2,1)S(1)}, u32[]{:S(2)}, u32[]{:S(2)}) collective-permute-start(bf16[8,64,512]{2,1,0:T(8,128)(2,1)S(1)} %gather_fusion.7), channel_id=1, source_target_pairs={{0,1},{1,2},{2,3},{3,0},{4,5},{5,6},{6,7},{7,4},{8,9},{9,10},{10,1... | collective-permute-start | bytes 1572872 | tf_op jit(solution)/shard_map/ppermute | solution.py:13
  172.2 15.0 %collective-permute-start.1 = (bf16[8,64,512]{2,1,0:T(8,128)(2,1)S(1)}, bf16[8,64,512]{2,1,0:T(8,128)(2,1)S(1)}, u32[]{:S(2)}, u32[]{:S(2)}) collective-permute-start(bf16[8,64,512]{2,1,0:T(8,128)(2,1)S(1)} %gather_fusion.7), channel_id=1, source_target_pairs={{1,0},{2,1},{3,2},{0,3},{5,4},{6,5},{7,6},{4,7},{9,8},{10,9},{11,1... | collective-permute-start | bytes 1572872 | tf_op jit(solution)/shard_map/ppermute | solution.py:16
  194.0 5.2 %copy-start.17 = (bf16[2,512,512]{2,1,0:T(8,128)(2,1)S(1)}, bf16[2,512,512]{2,1,0:T(8,128)(2,1)}, u32[]{:S(2)}) copy-start(bf16[2,512,512]{2,1,0:T(8,128)(2,1)} %param.38) | copy-start | bytes 3145732
  203.9 1.9 copy-start.6
  207.8 6.2 %copy-start.11 = (bf16[1,112,64,64]{1,3,2,0:T(8,128)(2,1)S(1)}, bf16[1,112,64,64]{1,3,2,0:T(8,128)(2,1)}, u32[]{:S(2)}) copy-start(bf16[1,112,64,64]{1,3,2,0:T(8,128)(2,1)} %get-tuple-element.20) | copy-start | bytes 2752516
  210.6 7.1 %copy-start.12 = (bf16[1024,512]{1,0:T(8,128)(2,1)}, bf16[1024,512]{1,0:T(8,128)(2,1)S(1)}, u32[]{:S(2)}) copy-start(bf16[1024,512]{1,0:T(8,128)(2,1)S(1)} %convolution_convert_fusion.1) | copy-start | bytes 3145732
  212.0 13.3 %collective-permute-start.2 = (bf16[8,64,512]{2,1,0:T(8,128)(2,1)}, bf16[8,64,512]{2,1,0:T(8,128)(2,1)}, u32[]{:S(2)}, u32[]{:S(2)}) collective-permute-start(bf16[8,64,512]{2,1,0:T(8,128)(2,1)} %gather_fusion.11), channel_id=1, source_target_pairs={{0,1},{1,2},{2,3},{3,0},{4,5},{5,6},{6,7},{7,4},{8,9},{9,10},{10,1... | collective-permute-start | bytes 1572872 | tf_op jit(solution)/shard_map/ppermute | solution.py:13
  212.3 14.5 %collective-permute-start.3 = (bf16[8,64,512]{2,1,0:T(8,128)(2,1)}, bf16[8,64,512]{2,1,0:T(8,128)(2,1)}, u32[]{:S(2)}, u32[]{:S(2)}) collective-permute-start(bf16[8,64,512]{2,1,0:T(8,128)(2,1)} %gather_fusion.11), channel_id=1, source_target_pairs={{1,0},{2,1},{3,2},{0,3},{5,4},{6,5},{7,6},{4,7},{9,8},{10,9},{11,1... | collective-permute-start | bytes 1572872 | tf_op jit(solution)/shard_map/ppermute | solution.py:16
  221.8 5.0 %copy-start.13 = (bf16[1024,512]{1,0:T(8,128)(2,1)S(1)}, bf16[1024,512]{1,0:T(8,128)(2,1)}, u32[]{:S(2)}) copy-start(bf16[1024,512]{1,0:T(8,128)(2,1)} %copy-done.12) | copy-start | bytes 3145732
  244.3 1.4 copy-start.7
  246.0 5.4 %copy-start.1 = (bf16[2048,512]{1,0:T(8,128)(2,1)S(1)}, bf16[2048,512]{1,0:T(8,128)(2,1)}, u32[]{:S(2)}) copy-start(bf16[2048,512]{1,0:T(8,128)(2,1)} %param.20) | copy-start | bytes 6291460
where the time goes:
time: 257 us; the launch traced here: 252 us
  local copies, waits for them, and re-layouts  103 us (40%)
  matrix products  52.7 us (21%)
  other arithmetic  47.3 us (18%)
  waiting for transfers between devices  31.7 us (12%)
  starting transfers between devices  15.8 us (6%)
    gather x7, local copies, waits for them, and re-layouts, aggregate(): slot_rows = source_table[padded_sources[slots]]  29.5 us
    dot_general x3, matrix products, aggregate(): jnp.einsum('bkij,bkid->bjd', slot_weight, slot_rows, preferred_element_ty...  20.3 us
    all_to_all x1, waiting for transfers between devices, on_device(): lax.all_to_all(outgoing, ('tile', 'dom'), split_axis=0, concat_axis=0, ti...  19.5 us
    unnamed x44, local copies, waits for them, and re-layouts  17.9 us
    scatter x2, local copies, waits for them, and re-layouts, aggregate(): jnp.full((blocks, width), tile_count, jnp.int32)  17.6 us
    dot_general x3, matrix products, update(): output_rows = jnp.dot(hidden, w_out, preferred_element_type=jnp.float32)  11.7 us
    all_to_all x1, starting transfers between devices, on_device(): lax.all_to_all(outgoing, ('tile', 'dom'), split_axis=0, concat_axis=0, ti...  11.7 us
    dot_general x3, matrix products, two_layer(): jnp.dot(hidden, w_out, preferred_element_type=jnp.float32)  11.1 us
  transfers between devices with their start and end apart: 5, of which 5 were waited for; matrix products, arithmetic and copies ran while one was open for 39% of the time, Pallas kernels for 0%

commit v1 on v0

v1 whole, which is shorter than its diff:
```python
import functools

import jax
import jax.numpy as jnp
from jax import lax
from jax.experimental import pallas as pl
from jax.experimental.pallas import tpu as pltpu
from jax.sharding import PartitionSpec as P

MESH = pl.DeviceIdType.MESH
F32 = jnp.float32
BF16 = jnp.bfloat16


def silu(v):
    half = 0.5 * v
    return half + half * jnp.tanh(half)


def mm(a, b):
    return jnp.dot(a, b, preferred_element_type=F32)


def pick(table, index):
    hit = index[:, None] == jnp.arange(table.shape[0], dtype=jnp.int32)[None, :]
    return jnp.sum(jnp.where(hit, table[None, :], 0), axis=1)


def invert(place):
    ids = jnp.arange(place.shape[0], dtype=jnp.int32)
    return jnp.sum(jnp.where(place[None, :] == ids[:, None], ids[None, :], 0), axis=1)


def grouped(group):
    count = group.shape[0]
    key = group * count + jnp.arange(count, dtype=jnp.int32)
    rank = jnp.sum((key[None, :] < key[:, None]).astype(jnp.int32), axis=1)
    return invert(rank)


def grid_kernel(send, latent, w_in, w_out, msg, outgoing):
    blocks, rows, width = latent.shape
    step = 4

    def mlp(i, _):
        at = pl.ds(i * step, step)
        x = latent[at].reshape(step * rows, width)
        h = silu(mm(x, w_in[...])).astype(BF16)
        msg[at] = mm(h, w_out[...]).astype(BF16).reshape(step, rows, width)
        return 0

    lax.fori_loop(0, blocks // step, mlp, 0)

    def put(i, _):
        for k in range(4):
            outgoing[i * 4 + k] = msg[send[i * 4 + k]]
        return 0

    lax.fori_loop(0, send.shape[0] // 4, put, 0)


def mesh_kernel(
    g_src, m_src, perm, place, halo_at,
    own, incoming, wt_g, wt_m, latent,
    e_in, e_out, e_gain, m_in, m_out, u_in, u_out, u_gain,
    out, table, state, mine, ptable0, ptable1, payload0, payload1, load_sem, send_sem, recv_sem,
):
    blocks, rows, width = latent.shape
    rim = halo_at.shape[0]
    ptable, payload = (ptable0, ptable1), (payload0, payload1)
    steps = wt_m.shape[0]
    n_dom = lax.axis_size("dom")
    x = lax.axis_index("dom")
    t = lax.axis_index("tile")
    upper = (t, lax.rem(x + 1, n_dom))
    lower = (t, lax.rem(x + n_dom - 1, n_dom))
    quarter = blocks // 4
    half_rim = rim // 2

    barrier = pltpu.get_barrier_semaphore()
    for peer in (lower, upper):
        pl.semaphore_signal(barrier, inc=1, device_id=peer, device_id_type=MESH)
    loads = [
        pltpu.make_async_copy(own, table.at[pl.ds(0, own.shape[0])], load_sem.at[0]),
        pltpu.make_async_copy(incoming, table.at[pl.ds(own.shape[0], incoming.shape[0])], load_sem.at[1]),
    ]
    for c in loads:
        c.start()
    pl.semaphore_wait(barrier, 2)
    for c in loads:
        c.wait()

    def halo(s, h):
        src = payload[s].at[pl.ds(h * half_rim, half_rim)]
        up = pltpu.make_async_remote_copy(
            src, ptable[s].at[pl.ds(blocks + h * half_rim, half_rim)],
            send_sem.at[s, 0, h], recv_sem.at[s, 0, h], device_id=upper, device_id_type=MESH)
        down = pltpu.make_async_remote_copy(
            src, ptable[s].at[pl.ds(blocks + rim + h * half_rim, half_rim)],
            send_sem.at[s, 1, h], recv_sem.at[s, 1, h], device_id=lower, device_id_type=MESH)
        return up, down

    def summed(tab, idx, wt, slots, c):
        parts = []
        for i in range(quarter):
            p = c * quarter + i
            got = jnp.concatenate([tab[idx[p * slots + k]] for k in range(slots)], axis=0)
            parts.append(mm(wt[p], got).astype(BF16))
        return jnp.concatenate(parts, axis=0)

    def update(old, agg, w_in, w_out, gain):
        pre = mm(old, w_in[pl.ds(0, width), :]) + mm(agg, w_in[pl.ds(width, width), :])
        o = mm(silu(pre).astype(BF16), w_out[...])
        mean = jnp.mean(o, axis=1, keepdims=True)
        cen = o - mean
        var = jnp.mean(cen * cen, axis=1, keepdims=True)
        normed = cen * lax.rsqrt(var + 1e-05) * gain
        return (old.astype(F32) + normed).astype(BF16)

    def message(s, c, new):
        h = silu(mm(new, m_in[s])).astype(BF16)
        msg = mm(h, m_out[s]).astype(BF16)
        msg = msg.reshape(quarter, rows, width)
        mine[pl.ds(c * quarter, quarter)] = msg
        ptable[s][pl.ds(c * quarter, quarter)] = msg

    def push(s, h):
        for i in range(half_rim):
            payload[s][h * half_rim + i] = mine[halo_at[h * half_rim + i]]
        for c in halo(s, h):
            c.start()

    slots_g = g_src.shape[0] // blocks
    slots_m = m_src.shape[0] // blocks

    def enc_chunk(c):
        agg = summed(table, g_src, wt_g, slots_g, c)
        old = jnp.concatenate([latent[perm[c * quarter + i]] for i in range(quarter)], axis=0)
        new = update(old, agg, e_in, e_out, e_gain[...])
        state[pl.ds(c * quarter, quarter)] = new.reshape(quarter, rows, width)
        message(0, c, new)

    def proc_chunk(s, c):
        agg = summed(ptable[s], m_src, wt_m.at[s], slots_m, c)
        old = state[pl.ds(c * quarter, quarter)].reshape(quarter * rows, width)
        new = update(old, agg, u_in.at[s], u_out.at[s], u_gain[pl.ds(s, 1), :])
        state[pl.ds(c * quarter, quarter)] = new.reshape(quarter, rows, width)
        if s + 1 < steps:
            message(s + 1, c, new)

    def rest(chunk, first):
        def body(c, _):
            chunk(c)
            return 0
        lax.fori_loop(first, 4, body, 0)

    enc_chunk(0)
    push(0, 0)
    enc_chunk(1)
    push(0, 1)
    rest(enc_chunk, 2)
    for s in range(steps):
        for h in range(2):
            for c in halo(s, h):
                c.wait()
        if s + 1 < steps:
            proc_chunk(s, 0)
            push(s + 1, 0)
            proc_chunk(s, 1)
            push(s + 1, 1)
            rest(functools.partial(proc_chunk, s), 2)
        else:
            rest(functools.partial(proc_chunk, s), 0)

    def restore(b, _):
        out[b] = state[place[b]]
        return 0

    lax.fori_loop(0, blocks, restore, 0)


def on_device(
    grid_latent, mesh_latent, g2m_send, g2m_src, g2m_dst, g2m_weight, halo_send, m2m_src, m2m_dst, m2m_weight,
    enc_msg_in, enc_msg_out, enc_upd_in, enc_upd_out, enc_gain,
    proc_msg_in, proc_msg_out, proc_upd_in, proc_upd_out, proc_gain,
):
    rows = g2m_weight.shape[1]
    width = grid_latent.shape[1]
    grid_blocks = grid_latent.shape[0] // rows
    blocks = mesh_latent.shape[0] // rows
    steps = proc_msg_in.shape[0]
    rim = halo_send.shape[1]
    peers = g2m_send.shape[1]
    vmem = pl.BlockSpec(memory_space=pltpu.VMEM)
    smem = pl.BlockSpec(memory_space=pltpu.SMEM)
    hbm = pl.BlockSpec(memory_space=pl.ANY)

    grid_msg, outgoing = pl.pallas_call(
        grid_kernel,
        out_shape=[
            jax.ShapeDtypeStruct((grid_blocks, rows, width), BF16),
            jax.ShapeDtypeStruct((peers, rows, width), BF16),
        ],
        in_specs=[smem, vmem, vmem, vmem],
        out_specs=[vmem, vmem],
        compiler_params=pltpu.CompilerParams(vmem_limit_bytes=32 * 2**20),
        name="grid_messages",
    )(g2m_send[0], grid_latent.reshape(grid_blocks, rows, width), enc_msg_in, enc_msg_out)
    incoming = lax.all_to_all(outgoing, ("tile", "dom"), split_axis=0, concat_axis=0, tiled=True)

    ids = jnp.arange(blocks, dtype=jnp.int32)
    named = halo_send[0][None, :] == ids[:, None]
    first = jnp.min(
        jnp.where(named, jnp.arange(rim, dtype=jnp.int32)[None, :], rim + ids[:, None]), axis=1
    )
    place = jnp.sum((first[None, :] < first[:, None]).astype(jnp.int32), axis=1)
    perm = invert(place)
    halo_at = pick(place, halo_send[0])
    g_order = grouped(pick(place, g2m_dst[0]))
    m_order = grouped(pick(place, m2m_dst[0]))
    g_src = pick(g2m_src[0], g_order)
    m_from = pick(m2m_src[0], m_order)
    m_src = jnp.where(m_from < blocks, pick(place, m_from), m_from)
    wt_g = jnp.transpose(
        g2m_weight[g_order].reshape(blocks, -1, rows, rows), (0, 3, 1, 2)
    ).reshape(blocks, rows, -1)
    wt_m = jnp.transpose(
        m2m_weight[:, m_order].reshape(steps, blocks, -1, rows, rows), (0, 1, 4, 2, 3)
    ).reshape(steps, blocks, rows, -1)

    out = pl.pallas_call(
        mesh_kernel,
        out_shape=jax.ShapeDtypeStruct((blocks, rows, width), BF16),
        in_specs=[smem] * 5 + [hbm, hbm] + [vmem] * 11,
        out_specs=vmem,
        scratch_shapes=[
            pltpu.VMEM((grid_blocks + peers, rows, width), BF16),
            pltpu.VMEM((blocks, rows, width), BF16),
            pltpu.VMEM((blocks, rows, width), BF16),
            pltpu.VMEM((blocks + 2 * rim, rows, width), BF16),
            pltpu.VMEM((blocks + 2 * rim, rows, width), BF16),
            pltpu.VMEM((rim, rows, width), BF16),
            pltpu.VMEM((rim, rows, width), BF16),
            pltpu.SemaphoreType.DMA((2,)),
            pltpu.SemaphoreType.DMA((steps, 2, 2)),
            pltpu.SemaphoreType.DMA((steps, 2, 2)),
        ],
        compiler_params=pltpu.CompilerParams(
            collective_id=0, has_side_effects=True, vmem_limit_bytes=48 * 2**20
        ),
        name="mesh_steps",
    )(
        g_src, m_src, perm, place, halo_at,
        grid_msg, incoming, wt_g, wt_m, mesh_latent.reshape(blocks, rows, width),
        enc_upd_in, enc_upd_out, enc_gain.reshape(1, width),
        proc_msg_in, proc_msg_out, proc_upd_in, proc_upd_out, proc_gain,
    )
    return out.reshape(blocks * rows, width)


def solution(mesh):
    both = P(("tile", "dom"), None)
    whole = P()
    placed = (
        both, both, both, both, both, P(("tile", "dom"), None, None), both, both, both,
        P(None, ("tile", "dom"), None, None),
    ) + (whole,) * 10
    return jax.shard_map(
        on_device, mesh=mesh, in_specs=placed, out_specs=both, check_vma=False
    )
```

time: 257 us -> 177 us (0.69)
  the two profiles are of different devices: /device:TPU:6 before, /device:TPU:1 now
where the time goes in v1:
time: 177 us; the launch traced here: 176 us
  waiting for transfers between devices  64.3 us (36%)
  local copies, waits for them, and re-layouts  49.8 us (28%)
  Pallas kernels  48.4 us (27%)
  starting transfers between devices  12 us (7%)
  other arithmetic  1.82 us (1%)
    all_to_all x1, waiting for transfers between devices, on_device(): lax.all_to_all(outgoing, ('tile', 'dom'), split_axis=0, concat_axis=0, ti...  64.3 us
    pallas_call x1, Pallas kernels, on_device(): pl.pallas_call(mesh_kernel, out_shape=jax.ShapeDtypeStruct((blocks, rows,...  42.6 us
    unnamed x43, local copies, waits for them, and re-layouts  22.4 us
    all_to_all x1, starting transfers between devices, on_device(): lax.all_to_all(outgoing, ('tile', 'dom'), split_axis=0, concat_axis=0, ti...  12 us
    reshape x1, local copies, waits for them, and re-layouts, on_device(): wt_m = jnp.transpose(m2m_weight[:, m_order].reshape(steps, blocks, -1, ro...  6.47 us
    transpose x1, local copies, waits for them, and re-layouts, on_device(): jnp.transpose(m2m_weight[:, m_order].reshape(steps, blocks, -1, rows, row...  6.42 us
    pallas_call x1, Pallas kernels, on_device(): pl.pallas_call(grid_kernel, out_shape=[jax.ShapeDtypeStruct((grid_blocks,...  5.79 us
    gather x1, local copies, waits for them, and re-layouts, on_device(): m2m_weight[:, m_order].reshape(steps, blocks, -1, rows, rows)  4.93 us
  transfers between devices with their start and end apart: 1, of which 1 were waited for; matrix products, arithmetic and copies ran while one was open for 22% of the time, Pallas kernels for 0%

profile of v1, /device:TPU:1, one launch (start us, length us, event | category | flops | bytes accessed | tf_op | source)
XLA Modules:
  0.0 176.4 jit_solution(13987277478640846267)
XLA Ops:
  0.0 0.0 copy-start.1
  0.0 1.6 copy-done.1
  1.6 0.0 copy-start.8
  1.6 1.0 copy-done.8
  2.6 0.0 copy-start.9
  2.6 1.0 copy-done.9
  3.7 0.0 copy-start.12
  3.7 0.7 copy-done.12
  4.3 5.8 %grid_messages.1 = (bf16[32,64,512]{2,1,0:T(8,128)(2,1)S(1)}, bf16[128,64,512]{2,1,0:T(8,128)(2,1)S(1)}) custom-call(s32[128]{0:T(128)S(1)} %bitcast.30, bf16[32,64,512]{2,1,0:T(8,128)(2,1)S(1)} %bitcast.27, bf16[512,512]{1,0:T(8,128)(2,1)S(1)} %copy-done.8, bf16[512,512]{1,0:T(8,128)(2,1)S(1)} %copy-done.9), custom_call_target="tpu_custom_call" | custom-call | tf_op jit(solution)/shard_map/grid_messages/pallas_call | solution.py:198
  10.1 0.0 copy-start
  10.1 3.2 %copy-done = bf16[128,64,512]{2,1,0:T(8,128)(2,1)} copy-done((bf16[128,64,512]{2,1,0:T(8,128)(2,1)}, bf16[128,64,512]{2,1,0:T(8,128)(2,1)S(1)}, u32[]{:S(2)}) %copy-start) | copy-done | bytes 8388632
  13.3 0.0 copy-start.2
  13.3 1.4 copy-done.2
  14.7 0.0 copy-start.13
  14.7 12.0 %all-to-all-start = ((bf16[128,64,512]{2,1,0:T(8,128)(2,1)}), bf16[128,64,512]{2,1,0:T(8,128)(2,1)}, u32[]{:S(2)}, u32[]{:S(2)}) async-start(bf16[128,64,512]{2,1,0:T(8,128)(2,1)} %copy-done), calls=%async_computation | async-start | bytes 16777216 | tf_op jit(solution)/shard_map/all_to_all | solution.py:209
  26.7 0.0 copy-done.13
  26.7 0.0 copy-start.18
  26.7 0.0 copy-start.16
  26.7 4.3 %copy.28 = bf16[224,64,64]{2,1,0:T(8,128)(2,1)} copy(bf16[224,64,64]{0,2,1:T(8,128)(2,1)S(1)} %copy-done.13) | data formatting | bytes 3670016 | tf_op args[5]
  31.0 0.0 copy-done.18
  31.0 0.1 select_reduce_fusion.9
  31.1 0.2 convert_reduce_fusion.2.place
  31.3 0.0 copy-done.16
  31.3 0.1 select_reduce_fusion.4
  31.4 0.2 convert_reduce_fusion
  31.6 0.1 select_reduce_fusion.1
  31.7 4.9 %gather_fusion = bf16[224,64,64]{2,1,0:T(8,128)(2,1)} fusion(bf16[224,64,64]{2,1,0:T(8,128)(2,1)} %copy.28, s32[1024]{0:T(1024)S(1)} %pad_clamp_fusion.1), kind=kCustom, calls=%fused_computation | custom fusion | bytes 3670912 | tf_op jit(solution)/shard_map/gather | solution.py:225
  36.7 0.0 copy-start.14
  36.7 4.7 %copy.33.wt_g = bf16[16,64,896]{2,1,0:T(8,128)(2,1)} copy(bf16[16,64,896]{1,2,0:T(8,128)(2,1)} %bitcast.31) | data formatting | bytes 3670016 | tf_op jit(solution)/shard_map/reshape | solution.py:226
  41.4 0.0 copy-done.14
  41.4 0.0 copy-start.17
  41.4 5.9 %copy.30 = bf16[2,112,64,64]{3,2,0,1:T(8,128)(2,1)} copy(bf16[2,112,64,64]{1,3,2,0:T(8,128)(2,1)S(1)} %copy-done.14) | data formatting | bytes 3670016 | tf_op args[9]
  47.2 0.0 copy-done.17
  47.2 0.1 select_reduce_fusion.7
  47.3 0.2 convert_reduce_fusion.1
  47.5 0.1 select_reduce_fusion.3
  47.6 4.9 %gather_fusion.1 = bf16[112,2,64,64]{3,2,1,0:T(8,128)(2,1)} fusion(bf16[2,112,64,64]{3,2,0,1:T(8,128)(2,1)} %copy.30, s32[1024]{0:T(1024)S(1)} %pad_clamp_fusion), kind=kCustom, calls=%fused_computation.1 | custom fusion | bytes 3670464 | tf_op jit(solution)/shard_map/gather | solution.py:228
  52.6 6.4 %copy.32 = bf16[2,16,64,7,64]{4,3,2,1,0:T(8,128)(2,1)} copy(bf16[2,16,64,7,64]{2,4,0,3,1:T(8,128)(2,1)} %bitcast.32) | data formatting | bytes 3670016 | tf_op jit(solution)/shard_map/transpose | solution.py:227
  59.0 0.0 copy-start.19
  59.0 0.0 copy-start.15
  59.0 0.0 copy-start.3
  59.0 0.0 copy-start.4
  59.0 0.0 copy-start.5
  59.0 0.0 copy-start.10
  59.0 0.0 copy-start.11
  59.0 6.5 %reshape.98.wt_m = bf16[2,16,64,448]{3,2,1,0:T(8,128)(2,1)} reshape(bf16[2,16,64,7,64]{4,3,2,1,0:T(8,128)(2,1)} %copy.32) | data formatting | bytes 3670016 | tf_op jit(solution)/shard_map/reshape | solution.py:229
  65.5 0.1 select_reduce_fusion.5.perm
  65.6 0.2 select_reduce_fusion.8.halo_at
  65.8 0.0 copy-done.19
  65.8 0.2 select_reduce_fusion.2
  66.0 0.1 select_reduce_fusion.6
  66.1 0.0 copy-done.15
  66.1 0.2 select_reduce_fusion.g_src
  66.3 64.3 %all-to-all-done.incoming = bf16[128,64,512]{2,1,0:T(8,128)(2,1)} async-done(((bf16[128,64,512]{2,1,0:T(8,128)(2,1)}), bf16[128,64,512]{2,1,0:T(8,128)(2,1)}, u32[]{:S(2)}, u32[]{:S(2)}) %all-to-all-start) | async-done | bytes 8388640 | tf_op jit(solution)/shard_map/all_to_all | solution.py:209
  130.5 0.0 copy-done.3
  130.5 0.0 copy-done.4
  130.5 0.0 copy-done.5
  130.5 0.0 copy-done.10
  130.6 0.0 copy-done.11
  130.6 0.0 copy-start.6
  130.6 1.2 copy-done.6
  131.8 1.0 copy-done.7
  132.8 42.6 %mesh_steps.1 = bf16[16,64,512]{2,1,0:T(8,128)(2,1)S(1)} custom-call(s32[224]{0:T(256)S(1)} %select_reduce_fusion.g_src, s32[112]{0:T(128)S(1)} %compare_select_fusion.2.m_src, s32[16]{0:T(128)S(1)} %select_reduce_fusion.5.perm, s32[16]{0:T(128)S(1)} %convert_reduce_fusion.2.place, s32[8]{0:T(128)S(1)} %select_reduce_fusion.8.halo_at, ...), custom_call_target="tpu_custom_call" | custom-call | tf_op jit(solution)/shard_map/mesh_steps/pallas_call | solution.py:231
  175.5 1.0 copy.36
  (9 shorter events, 0.0 us)
Async XLA Ops:
  0.0 1.6 copy-start.1
  1.6 1.0 copy-start.8
  2.6 1.0 copy-start.9
  3.7 0.7 copy-start.12
  10.1 3.2 %copy-start = (bf16[128,64,512]{2,1,0:T(8,128)(2,1)}, bf16[128,64,512]{2,1,0:T(8,128)(2,1)S(1)}, u32[]{:S(2)}) copy-start(bf16[128,64,512]{2,1,0:T(8,128)(2,1)S(1)} %get-tuple-element.8) | copy-start | bytes 25165828
  13.3 1.4 copy-start.2
  14.7 12.0 %copy-start.13 = (bf16[224,64,64]{0,2,1:T(8,128)(2,1)S(1)}, bf16[224,64,64]{0,2,1:T(8,128)(2,1)}, u32[]{:S(2)}) copy-start(bf16[224,64,64]{0,2,1:T(8,128)(2,1)} %param.25) | copy-start | bytes 5505028
  14.7 115.8 %all-to-all-start = ((bf16[128,64,512]{2,1,0:T(8,128)(2,1)}), bf16[128,64,512]{2,1,0:T(8,128)(2,1)}, u32[]{:S(2)}, u32[]{:S(2)}) async-start(bf16[128,64,512]{2,1,0:T(8,128)(2,1)} %copy-done), calls=%async_computation | async-start | bytes 16777216 | tf_op jit(solution)/shard_map/all_to_all | solution.py:209
  26.7 4.3 %copy-start.18 = (s32[1,8]{1,0:T(1,128)S(1)}, s32[1,8]{1,0:T(1,128)}, u32[]{:S(2)}) copy-start(s32[1,8]{1,0:T(1,128)} %param.26) | copy-start | bytes 100
  26.7 4.6 %copy-start.16 = (s32[1,224]{1,0:T(1,128)S(1)}, s32[1,224]{1,0:T(1,128)}, u32[]{:S(2)}) copy-start(s32[1,224]{1,0:T(1,128)} %param.24) | copy-start | bytes 2692
  36.7 4.7 %copy-start.14 = (bf16[2,112,64,64]{1,3,2,0:T(8,128)(2,1)S(1)}, bf16[2,112,64,64]{1,3,2,0:T(8,128)(2,1)}, u32[]{:S(2)}) copy-start(bf16[2,112,64,64]{1,3,2,0:T(8,128)(2,1)} %param.29) | copy-start | bytes 5505028
  41.4 5.9 %copy-start.17 = (s32[1,112]{1,0:T(1,128)S(1)}, s32[1,112]{1,0:T(1,128)}, u32[]{:S(2)}) copy-start(s32[1,112]{1,0:T(1,128)} %param.28) | copy-start | bytes 1348
  59.0 6.8 %copy-start.19 = (s32[1,112]{1,0:T(1,128)S(1)}, s32[1,112]{1,0:T(1,128)}, u32[]{:S(2)}) copy-start(s32[1,112]{1,0:T(1,128)} %param.27) | copy-start | bytes 1348
  59.0 7.1 %copy-start.15 = (s32[1,224]{1,0:T(1,128)S(1)}, s32[1,224]{1,0:T(1,128)}, u32[]{:S(2)}) copy-start(s32[1,224]{1,0:T(1,128)} %param.23) | copy-start | bytes 2692
  59.0 71.6 %copy-start.3 = (bf16[1024,512]{1,0:T(8,128)(2,1)S(1)}, bf16[1024,512]{1,0:T(8,128)(2,1)}, u32[]{:S(2)}) copy-start(bf16[1024,512]{1,0:T(8,128)(2,1)} %param.21) | copy-start | bytes 3145732
  59.0 71.6 %copy-start.4 = (bf16[1024,512]{1,0:T(8,128)(2,1)S(1)}, bf16[1024,512]{1,0:T(8,128)(2,1)}, u32[]{:S(2)}) copy-start(bf16[1024,512]{1,0:T(8,128)(2,1)} %e_in.1) | copy-start | bytes 3145732
  59.0 71.5 %copy-start.5 = (bf16[2,512,512]{2,1,0:T(8,128)(2,1)S(1)}, bf16[2,512,512]{2,1,0:T(8,128)(2,1)}, u32[]{:S(2)}) copy-start(bf16[2,512,512]{2,1,0:T(8,128)(2,1)} %m_in.1) | copy-start | bytes 3145732
  59.0 71.5 %copy-start.10 = (f32[2,512]{1,0:T(2,128)S(1)}, f32[2,512]{1,0:T(2,128)}, u32[]{:S(2)}) copy-start(f32[2,512]{1,0:T(2,128)} %u_gain.1) | copy-start | bytes 12292
  59.0 71.5 %copy-start.11 = (f32[512]{0:T(512)S(1)}, f32[512]{0:T(512)}, u32[]{:S(2)}) copy-start(f32[512]{0:T(512)} %param.34) | copy-start | bytes 6148
  130.6 1.2 copy-start.6
  131.8 1.0 copy-start.7

commit v2 on v1

v2 whole, which is shorter than its diff:
```python
import functools

import jax
import jax.numpy as jnp
from jax import lax
from jax.experimental import pallas as pl
from jax.experimental.pallas import tpu as pltpu
from jax.sharding import PartitionSpec as P

MESH = pl.DeviceIdType.MESH
F32 = jnp.float32
BF16 = jnp.bfloat16


def silu(v):
    half = 0.5 * v
    return half + half * jnp.tanh(half)


def mm(a, b):
    return jnp.dot(a, b, preferred_element_type=F32)


def pick(table, index):
    hit = index[:, None] == jnp.arange(table.shape[0], dtype=jnp.int32)[None, :]
    return jnp.sum(jnp.where(hit, table[None, :], 0), axis=1)


def invert(place):
    ids = jnp.arange(place.shape[0], dtype=jnp.int32)
    return jnp.sum(jnp.where(place[None, :] == ids[:, None], ids[None, :], 0), axis=1)


def grouped(group):
    count = group.shape[0]
    key = group * count + jnp.arange(count, dtype=jnp.int32)
    rank = jnp.sum((key[None, :] < key[:, None]).astype(jnp.int32), axis=1)
    return invert(rank)


PARTS = 4
LINES = (("x", "y", "z"), ("y", "z", "x"), ("z", "x", "y"), ("x", "y", "z"))
AXES = ("x", "y", "z")


def whole_kernel(
    g_order, g_src, m_order, m_src, perm, place, halo_at,
    send_row, grid_latent, latent_in, g_weight, m_weight,
    a_in_h, a_out_h, e_in_h, e_out_h, e_gain, m_in_h, m_out_h, u_in_h, u_out_h, u_gain,
    out_h,
    grid_x, a_in, a_out, e_in, e_out, m_in, m_out, u_in, u_out, latent,
    raw, wt_g, wt_m, table, ag0, ag1, ag2, ag3, s0, s1, s2, r0, r1, r2, r3,
    state, mine, ptable0, ptable1, payload0, payload1, own_row, rows_v, rows_s,
    chunk_sem, load_sem, row_s, row_r, ag_s, ag_r, relay_s, relay_r, mid_s, mid_r, last_s, last_r, local_sem,
    send_sem, recv_sem,
):
    blocks, rows, width = latent.shape
    grid_blocks = grid_x.shape[0]
    sub = rows // PARTS
    rim = halo_at.shape[0]
    steps = m_in.shape[0]
    ptable, payload = (ptable0, ptable1), (payload0, payload1)
    ag, stage, held = (ag0, ag1, ag2, ag3), (s0, s1, s2, s0), (r0, r1, r2, r3)
    tile = lax.axis_index("tile")
    core = lax.rem(tile, 2)
    at = {"x": lax.axis_index("dom"), "y": lax.rem(tile // 2, 4), "z": tile // 8}

    def device(c, core_at):
        return (c["z"] * 4 + c["y"]) * 2 + core_at, c["x"]

    def moved(axis, by, flip=0):
        c = dict(at)
        c[axis] = lax.rem(at[axis] + by + 4, 4)
        return device(c, lax.rem(core + flip, 2))

    chunk = 4
    chunks = grid_blocks // chunk

    def chunk_load(i):
        return pltpu.make_async_copy(
            grid_latent.at[pl.ds(i * chunk, chunk)], grid_x.at[pl.ds(i * chunk, chunk)], chunk_sem.at[i])

    loads = [
        pltpu.make_async_copy(src, dst, load_sem.at[i])
        for i, (src, dst) in enumerate((
            (a_in_h, a_in), (a_out_h, a_out), (send_row, own_row), (g_weight, raw), (latent_in, latent),
            (e_in_h, e_in), (e_out_h, e_out), (m_in_h, m_in), (m_out_h, m_out), (u_in_h, u_in), (u_out_h, u_out),
        ))
    ]
    loads[0].start()
    chunk_load(0).start()
    loads[1].start()
    loads[2].start()
    for i in range(1, chunks):
        chunk_load(i).start()
    for c in loads[3:]:
        c.start()

    barrier = pltpu.get_barrier_semaphore()
    greeted = [moved(axis, by, flip) for axis in AXES for by in (1, 2, 3) for flip in (0, 1)] + [moved("x", 0, 1)]
    for peer in greeted:
        pl.semaphore_signal(barrier, inc=1, device_id=peer, device_id_type=MESH)

    def mlp(i, _):
        chunk_load(i).wait()
        x = grid_x[pl.ds(i * chunk, chunk)].reshape(chunk * rows, width)
        h = silu(mm(x, a_in[...])).astype(BF16)
        msg = mm(h, a_out[...]).astype(BF16).reshape(chunk, rows, width)
        table[0, i // 2, lax.rem(i, 2)] = msg
        for p in range(PARTS):
            ag[p][at[LINES[p][0]], pl.ds(i * chunk, chunk)] = msg[:, p * sub:(p + 1) * sub]
        return 0

    half = grid_blocks // 2

    def gather_copy(p, way, h):
        axis = LINES[p][0]
        ref = ag[p].at[at[axis], pl.ds(h * half, half)]
        return pltpu.make_async_remote_copy(
            ref, ref, ag_s.at[p, way, h], ag_r.at[p, way, h],
            device_id=moved(axis, 1 - 2 * way), device_id_type=MESH)

    def relay_copy(p, way):
        axis = LINES[p][0]
        by = 1 - 2 * way
        ref = ag[p].at[lax.rem(at[axis] - by + 4, 4), pl.ds(way * half, half)]
        return pltpu.make_async_remote_copy(
            ref, ref, relay_s.at[p, way], relay_r.at[p, way],
            device_id=moved(axis, by), device_id_type=MESH)

    def row_copy(a, by):
        axis = AXES[a]
        return pltpu.make_async_remote_copy(
            own_row, rows_v.at[a, at[axis]], row_s.at[a, by - 1], row_r.at[a, by - 1],
            device_id=moved(axis, by), device_id_type=MESH)

    loads[0].wait()
    loads[1].wait()
    lax.fori_loop(0, chunks // 2, mlp, 0)
    pl.semaphore_wait(barrier, len(greeted))
    for p in range(3):
        for way in (0, 1):
            gather_copy(p, way, 0).start()
    loads[2].wait()
    for a in range(3):
        for by in (1, 2, 3):
            row_copy(a, by).start()
    own_rows = [pltpu.make_async_copy(own_row, rows_v.at[a, at[AXES[a]]], local_sem.at[a]) for a in range(3)]
    for c in own_rows:
        c.start()
    lax.fori_loop(chunks // 2, chunks, mlp, 0)
    for p in range(3):
        for way in (0, 1):
            gather_copy(p, way, 1).start()

    def relays(p):
        for way in (0, 1):
            gather_copy(p, way, way).wait_recv()
            relay_copy(p, way).start()

    def gathered(p):
        for way in (0, 1):
            gather_copy(p, way, 1 - way).wait_recv()
            relay_copy(p, way).wait_recv()

    def held_at(p, b):
        return held[p].at[:, b] if p == 2 else held[p].at[b]

    def mid_copy(p, by):
        axis = LINES[p][1]
        return pltpu.make_async_remote_copy(
            stage[p].at[by - 1], held_at(p, at[axis]), mid_s.at[p, by - 1], mid_r.at[p, by - 1],
            device_id=moved(axis, by), device_id_type=MESH)

    def select(p):
        first, second, third = LINES[p]
        a = AXES.index(first)

        def of(by, j):
            c = dict(at)
            c[second] = lax.rem(at[second] + by, 4)
            for k in range(8):
                c[third] = k // 2
                t, x = device(c, k % 2)
                got = ag[p][j, rows_s[a, j, 0, t * 4 + x]]
                yield k // 2, k % 2, got

        def keep(j, _):
            for c3, k, got in of(0, j):
                if p == 2:
                    held[p][j, at[second], c3, k] = got
                else:
                    held[p][at[second], j, c3, k] = got
            return 0

        def put(i, _):
            by, j = 1 + i // 4, lax.rem(i, 4)
            for c3, k, got in of(by, j):
                stage[p][by - 1, j, c3, k] = got
            return 0

        lax.fori_loop(0, 12, put, 0)
        for by in (1, 2, 3):
            mid_copy(p, by).start()
        lax.fori_loop(0, 4, keep, 0)

    def arrived(p):
        for by in (1, 2, 3):
            mid_copy(p, by).wait_recv()

    def landing(p):
        here = pl.ds(p * sub, sub)
        if p == 1:
            return table.at[pl.ds(1, 4), :, core, at["x"], here]
        if p == 2:
            return table.at[pl.ds(1, 4), at["y"], core, :, here]
        return table.at[1 + at["z"], :, core, :, here]

    others = [(by, flip) for by in (1, 3, 2, 0) for flip in (0, 1) if by or flip]

    def last_copy(p, by, flip):
        axis = LINES[p][2]
        return pltpu.make_async_remote_copy(
            held[p].at[:, :, lax.rem(at[axis] + by, 4), lax.rem(core + flip, 2)], landing(p),
            last_s.at[p, by, flip], last_r.at[p, by, flip],
            device_id=moved(axis, by, flip), device_id_type=MESH)

    def keep_copy(p):
        return pltpu.make_async_copy(held[p].at[:, :, at[LINES[p][2]], core], landing(p), local_sem.at[3 + p])

    def deliver(p):
        for by, flip in others:
            last_copy(p, by, flip).start()
        keep_copy(p).start()

    slots_g = g_src.shape[0] // blocks
    slots_m = m_src.shape[0] // blocks

    def prepare(order, base, wt, slots):
        def body(b, _):
            cat = jnp.concatenate([raw[base + order[b * slots + k]] for k in range(slots)], axis=0)
            wt[b] = cat.T
            return 0
        lax.fori_loop(0, blocks, body, 0)

    for p in range(3):
        relays(p)
    for a in range(3):
        own_rows[a].wait()
        for by in (1, 2, 3):
            row_copy(a, by).wait()
    to_scalar = pltpu.make_async_copy(rows_v, rows_s, local_sem.at[0])
    to_scalar.start()
    to_scalar.wait()

    gathered(0)
    for h in (0, 1):
        for way in (0, 1):
            gather_copy(3, way, h).start()
    select(0)
    gathered(1)
    select(1)
    gathered(2)
    loads[3].wait()
    prepare(g_order, 0, wt_g, slots_g)
    m_load = pltpu.make_async_copy(m_weight, raw, load_sem.at[3])
    m_load.start()
    relays(3)
    gathered(3)
    select(2)
    arrived(0)
    for by in (1, 2, 3):
        mid_copy(0, by).wait_send()
    select(3)
    deliver(0)
    m_load.wait()
    for s in range(steps):
        prepare(m_order, s * (raw.shape[0] // steps), wt_m.at[s], slots_m)
    arrived(1)
    arrived(2)
    deliver(1)
    deliver(2)
    arrived(3)
    deliver(3)
    for c in loads[4:]:
        c.wait()
    for p in range(PARTS):
        for by, flip in others:
            last_copy(p, by, flip).wait_recv()
        keep_copy(p).wait()

    n_dom = lax.axis_size("dom")
    upper, lower = moved("x", 1), moved("x", 3)
    quarter = blocks // 4
    half_rim = rim // 2

    def halo(s, h):
        src = payload[s].at[pl.ds(h * half_rim, half_rim)]
        up = pltpu.make_async_remote_copy(
            src, ptable[s].at[pl.ds(blocks + h * half_rim, half_rim)],
            send_sem.at[s, 0, h], recv_sem.at[s, 0, h], device_id=upper, device_id_type=MESH)
        down = pltpu.make_async_remote_copy(
            src, ptable[s].at[pl.ds(blocks + rim + h * half_rim, half_rim)],
            send_sem.at[s, 1, h], recv_sem.at[s, 1, h], device_id=lower, device_id_type=MESH)
        return up, down

    def from_grid(i):
        return table[i // 32, lax.rem(i // 8, 4), lax.rem(i // 4, 2), lax.rem(i, 4)]

    def summed(load, idx, wt, slots, c):
        parts = []
        for i in range(quarter):
            p = c * quarter + i
            got = jnp.concatenate([load(idx[p * slots + k]) for k in range(slots)], axis=0)
            parts.append(mm(wt[p], got).astype(BF16))
        return jnp.concatenate(parts, axis=0)

    def update(old, agg, w_in, w_out, gain):
        pre = mm(old, w_in[pl.ds(0, width), :]) + mm(agg, w_in[pl.ds(width, width), :])
        o = mm(silu(pre).astype(BF16), w_out[...])
        mean = jnp.mean(o, axis=1, keepdims=True)
        cen = o - mean
        var = jnp.mean(cen * cen, axis=1, keepdims=True)
        normed = cen * lax.rsqrt(var + 1e-05) * gain
        return (old.astype(F32) + normed).astype(BF16)

    def message(s, c, new):
        h = silu(mm(new, m_in[s])).astype(BF16)
        msg = mm(h, m_out[s]).astype(BF16)
        msg = msg.reshape(quarter, rows, width)
        mine[pl.ds(c * quarter, quarter)] = msg
        ptable[s][pl.ds(c * quarter, quarter)] = msg

    def push(s, h):
        for i in range(half_rim):
            payload[s][h * half_rim + i] = mine[halo_at[h * half_rim + i]]
        for c in halo(s, h):
            c.start()

    def enc_chunk(c):
        agg = summed(from_grid, g_src, wt_g, slots_g, c)
        old = jnp.concatenate([latent[perm[c * quarter + i]] for i in range(quarter)], axis=0)
        new = update(old, agg, e_in, e_out, e_gain[...])
        state[pl.ds(c * quarter, quarter)] = new.reshape(quarter, rows, width)
        message(0, c, new)

    def proc_chunk(s, c):
        agg = summed(lambda i: ptable[s][i], m_src, wt_m.at[s], slots_m, c)
        old = state[pl.ds(c * quarter, quarter)].reshape(quarter * rows, width)
        new = update(old, agg, u_in.at[s], u_out.at[s], u_gain[pl.ds(s, 1), :])
        state[pl.ds(c * quarter, quarter)] = new.reshape(quarter, rows, width)
        if s + 1 < steps:
            message(s + 1, c, new)

    def rest(chunk, first):
        def body(c, _):
            chunk(c)
            return 0
        lax.fori_loop(first, 4, body, 0)

    enc_chunk(0)
    push(0, 0)
    enc_chunk(1)
    push(0, 1)
    rest(enc_chunk, 2)
    for s in range(steps):
        for h in range(2):
            for c in halo(s, h):
                c.wait()
        if s + 1 < steps:
            proc_chunk(s, 0)
            push(s + 1, 0)
            proc_chunk(s, 1)
            push(s + 1, 1)
            rest(functools.partial(proc_chunk, s), 2)
        else:
            rest(functools.partial(proc_chunk, s), 0)

    def restore(b, _):
        mine[b] = state[place[b]]
        return 0

    lax.fori_loop(0, blocks, restore, 0)
    store = pltpu.make_async_copy(mine, out_h, local_sem.at[0])
    store.start()
    for p in range(PARTS):
        for way in (0, 1):
            relay_copy(p, way).wait_send()
            for h in (0, 1):
                gather_copy(p, way, h).wait_send()
        for by, flip in others:
            last_copy(p, by, flip).wait_send()
        if p:
            for by in (1, 2, 3):
                mid_copy(p, by).wait_send()
    store.wait()


def on_device(
    grid_latent, mesh_latent, g2m_send, g2m_src, g2m_dst, g2m_weight, halo_send, m2m_src, m2m_dst, m2m_weight,
    enc_msg_in, enc_msg_out, enc_upd_in, enc_upd_out, enc_gain,
    proc_msg_in, proc_msg_out, proc_upd_in, proc_upd_out, proc_gain,
):
    rows = g2m_weight.shape[1]
    width = grid_latent.shape[1]
    grid_blocks = grid_latent.shape[0] // rows
    blocks = mesh_latent.shape[0] // rows
    steps = proc_msg_in.shape[0]
    rim = halo_send.shape[1]
    peers = g2m_send.shape[1]
    vmem = pl.BlockSpec(memory_space=pltpu.VMEM)
    smem = pl.BlockSpec(memory_space=pltpu.SMEM)
    hbm = pl.BlockSpec(memory_space=pl.ANY)

    ids = jnp.arange(blocks, dtype=jnp.int32)
    named = halo_send[0][None, :] == ids[:, None]
    first = jnp.min(
        jnp.where(named, jnp.arange(rim, dtype=jnp.int32)[None, :], rim + ids[:, None]), axis=1
    )
    place = jnp.sum((first[None, :] < first[:, None]).astype(jnp.int32), axis=1)
    perm = invert(place)
    halo_at = pick(place, halo_send[0])
    g_order = grouped(pick(place, g2m_dst[0]))
    m_order = grouped(pick(place, m2m_dst[0]))
    g_src = pick(g2m_src[0], g_order)
    m_from = pick(m2m_src[0], m_order)
    m_src = jnp.where(m_from < blocks, pick(place, m_from), m_from)
    sub = rows // PARTS
    flying = (4, grid_blocks, sub, width)
    staged = (3, 4, 4, 2, sub, width)
    holding = (4, 4, 4, 2, sub, width)
    dma = pltpu.SemaphoreType.DMA
    vm = pltpu.VMEM
    out = pl.pallas_call(
        whole_kernel,
        out_shape=jax.ShapeDtypeStruct((blocks, rows, width), BF16),
        in_specs=[smem] * 7 + [hbm] * 9 + [vmem] + [hbm] * 4 + [vmem],
        out_specs=hbm,
        scratch_shapes=[
            vm((grid_blocks, rows, width), BF16),
            *[vm(w.shape, BF16) for w in (
                enc_msg_in, enc_msg_out, enc_upd_in, enc_upd_out,
                proc_msg_in, proc_msg_out, proc_upd_in, proc_upd_out)],
            vm((blocks, rows, width), BF16),
            vm(g2m_weight.shape, BF16),
            vm((blocks, rows, rows * (g2m_dst.shape[1] // blocks)), BF16),
            vm((steps, blocks, rows, rows * (m2m_dst.shape[1] // blocks)), BF16),
            vm((5, 4, 2, 4, rows, width), BF16),
            *[vm(flying, BF16)] * 4,
            *[vm(staged, BF16)] * 3,
            *[vm(holding, BF16)] * 4,
            vm((blocks, rows, width), BF16),
            vm((blocks, rows, width), BF16),
            vm((blocks + 2 * rim, rows, width), BF16),
            vm((blocks + 2 * rim, rows, width), BF16),
            vm((rim, rows, width), BF16),
            vm((rim, rows, width), BF16),
            vm((1, peers), jnp.int32),
            vm((3, 4, 1, peers), jnp.int32),
            pltpu.SMEM((3, 4, 1, peers), jnp.int32),
            dma((8,)), dma((11,)), dma((3, 3)), dma((3, 3)),
            dma((4, 2, 2)), dma((4, 2, 2)), dma((4, 2)), dma((4, 2)),
            dma((4, 3)), dma((4, 3)), dma((4, 4, 2)), dma((4, 4, 2)), dma((7,)),
            dma((steps, 2, 2)), dma((steps, 2, 2)),
        ],
        compiler_params=pltpu.CompilerParams(
            collective_id=0, has_side_effects=True, vmem_limit_bytes=62 * 2**20
        ),
        name="encoder_and_steps",
    )(
        g_order, g_src, m_order, m_src, perm, place, halo_at,
        g2m_send, grid_latent.reshape(grid_blocks, rows, width), mesh_latent.reshape(blocks, rows, width),
        g2m_weight, m2m_weight.reshape(g2m_weight.shape),
        enc_msg_in, enc_msg_out, enc_upd_in, enc_upd_out, enc_gain.reshape(1, width),
        proc_msg_in, proc_msg_out, proc_upd_in, proc_upd_out, proc_gain,
    )
    return out.reshape(blocks * rows, width)


def solution(mesh):
    both = P(("tile", "dom"), None)
    whole = P()
    placed = (
        both, both, both, both, both, P(("tile", "dom"), None, None), both, both, both,
        P(None, ("tile", "dom"), None, None),
    ) + (whole,) * 10
    return jax.shard_map(
        on_device, mesh=mesh, in_specs=placed, out_specs=both, check_vma=False
    )
```

time: 177 us -> 161 us (0.910)
  Pallas kernels: 48.4 us -> 137 us
  waiting for transfers between devices: 64.3 us -> 0 us
  local copies, waits for them, and re-layouts: 49.8 us -> 14 us
  starting transfers between devices: 12 us -> 0 us
  other arithmetic: 1.82 us -> 7.94 us
    pallas_call x2 -> x1, Pallas kernels: 48.4 us -> 137 us  [on_device(): pl.pallas_call(whole_kernel, out_shape=jax.ShapeDtypeStruct((blocks, rows...]
    all_to_all x1 -> x0, waiting for transfers between devices: 64.3 us -> none  [on_device(): lax.all_to_all(outgoing, ('tile', 'dom'), split_axis=0, concat_axis=0, ti...]
    all_to_all x1 -> x0, starting transfers between devices: 12 us -> none  [on_device(): lax.all_to_all(outgoing, ('tile', 'dom'), split_axis=0, concat_axis=0, ti...]
    reshape x2 -> x0, local copies, waits for them, and re-layouts: 11.2 us -> none  [the longest x1 6.47 us: on_device(): wt_m = jnp.transpose(m2m_weight[:, m_order].reshape(steps, blocks, -1, ro...]
    gather x2 -> x0, local copies, waits for them, and re-layouts: 9.84 us -> none  [the longest x1 4.93 us: on_device(): m2m_weight[:, m_order].reshape(steps, blocks, -1, rows, rows)]
    unnamed x43 -> x11, local copies, waits for them, and re-layouts: 22.4 us -> 14 us
    transpose x1 -> x0, local copies, waits for them, and re-layouts: 6.42 us -> none  [on_device(): jnp.transpose(m2m_weight[:, m_order].reshape(steps, blocks, -1, rows, row...]
    reduce_sum x6, other arithmetic: 0.8 us -> 5.24 us  [pick(): return jnp.sum(jnp.where(hit, table[None, :], 0), axis=1)]
  transfers between devices with their start and end apart: 1 -> 0, of which waited for: 1 -> 0; matrix products, arithmetic and copies ran while one was open for 22% -> 0% of each run, Pallas kernels for 0% -> 0%
where the time goes in v2:
time: 161 us; the launch traced here: 159 us
  Pallas kernels  137 us (85%)
  local copies, waits for them, and re-layouts  14 us (9%)
  other arithmetic  7.94 us (5%)
    pallas_call x1, Pallas kernels, on_device(): pl.pallas_call(whole_kernel, out_shape=jax.ShapeDtypeStruct((blocks, rows...  137 us
    unnamed x11, local copies, waits for them, and re-layouts  14 us
    reduce_sum x6, other arithmetic, pick(): return jnp.sum(jnp.where(hit, table[None, :], 0), axis=1)  5.24 us

profile of v2, /device:TPU:1, one launch (start us, length us, event | category | flops | bytes accessed | tf_op | source)
XLA Modules:
  0.0 158.9 jit_solution(8924905383330067346)
XLA Ops:
  0.0 0.7 select_reduce_fusion.9
  0.7 0.2 convert_reduce_fusion.2.place
  0.9 0.0 copy-start.2
  0.9 1.4 select_reduce_fusion.8.halo_at
  2.3 0.6 select_reduce_fusion.5.perm
  3.0 0.7 select_reduce_fusion.7
  3.7 0.2 convert_reduce_fusion.1
  3.9 0.1 select_reduce_fusion.3.m_order
  4.0 0.0 copy-start.3
  4.0 0.8 select_reduce_fusion.2
  4.9 0.1 select_reduce_fusion.6
  5.0 0.5 compare_select_fusion.m_src
  5.5 0.8 select_reduce_fusion.4
  6.3 0.2 convert_reduce_fusion
  6.5 0.1 select_reduce_fusion.1.g_order
  6.6 0.0 copy-start.1
  6.6 1.4 select_reduce_fusion.g_src
  8.0 0.0 copy-start
  8.0 5.8 %copy.24.g_weight = bf16[224,64,64]{2,1,0:T(8,128)(2,1)} copy(bf16[224,64,64]{0,2,1:T(8,128)(2,1)} %param.25) | data formatting | bytes 3670016 | tf_op args[5]
  13.8 0.0 copy-done.2
  13.8 0.0 copy-done.3
  13.8 0.0 copy-done.1
  13.8 0.0 copy-done
  13.8 5.9 %copy.23 = bf16[2,112,64,64]{3,2,1,0:T(8,128)(2,1)} copy(bf16[2,112,64,64]{1,3,2,0:T(8,128)(2,1)S(1)} %copy-done) | data formatting | bytes 3670016 | tf_op args[9]
  19.7 136.9 %encoder_and_steps.1 = bf16[16,64,512]{2,1,0:T(8,128)(2,1)} custom-call(s32[224]{0:T(256)} %copy-done.1, s32[224]{0:T(256)} %select_reduce_fusion.g_src, s32[112]{0:T(128)} %copy-done.3, s32[112]{0:T(128)} %compare_select_fusion.m_src, s32[16]{0:T(128)} %select_reduce_fusion.5.perm, s32[16]{0:T(128)} %copy-done.2, s32[8]{0:T(128)} %select_reduce_fusion.8.halo_at, ...), custom_call_target="tpu_custom_call" | custom-call | tf_op jit(solution)/shard_map/encoder_and_steps/pallas_call | solution.py:434
  156.7 2.3 %copy.26 = bf16[1024,512]{1,0:T(8,128)(2,1)} copy(bf16[1024,512]{1,0:T(8,128)(2,1)} %bitcast.11) | data formatting | bytes 2097152
  (3 shorter events, 0.0 us)
Async XLA Ops:
  0.9 12.8 %copy-start.2 = (s32[16]{0:T(128)}, s32[16]{0:T(128)S(1)}, u32[]{:S(2)}) copy-start(s32[16]{0:T(128)S(1)} %convert_reduce_fusion.2.place) | copy-start | bytes 196
  4.0 9.7 %copy-start.3 = (s32[112]{0:T(128)}, s32[112]{0:T(128)S(1)}, u32[]{:S(2)}) copy-start(s32[112]{0:T(128)S(1)} %select_reduce_fusion.3.m_order) | copy-start | bytes 1348
  6.6 7.2 %copy-start.1 = (s32[224]{0:T(256)}, s32[224]{0:T(256)S(1)}, u32[]{:S(2)}) copy-start(s32[224]{0:T(256)S(1)} %select_reduce_fusion.1.g_order) | copy-start | bytes 2692
  8.0 5.8 %copy-start = (bf16[2,112,64,64]{1,3,2,0:T(8,128)(2,1)S(1)}, bf16[2,112,64,64]{1,3,2,0:T(8,128)(2,1)}, u32[]{:S(2)}) copy-start(bf16[2,112,64,64]{1,3,2,0:T(8,128)(2,1)} %param.29) | copy-start | bytes 5505028

commit v3 on v2

--- a/solution.py
+++ b/solution.py
@@ -21,21 +21,33 @@
     return jnp.dot(a, b, preferred_element_type=F32)
 
 
-def pick(table, index):
-    hit = index[:, None] == jnp.arange(table.shape[0], dtype=jnp.int32)[None, :]
-    return jnp.sum(jnp.where(hit, table[None, :], 0), axis=1)
-
-
-def invert(place):
-    ids = jnp.arange(place.shape[0], dtype=jnp.int32)
-    return jnp.sum(jnp.where(place[None, :] == ids[:, None], ids[None, :], 0), axis=1)
-
-
-def grouped(group):
-    count = group.shape[0]
-    key = group * count + jnp.arange(count, dtype=jnp.int32)
-    rank = jnp.sum((key[None, :] < key[:, None]).astype(jnp.int32), axis=1)
-    return invert(rank)
+def iota(shape, dim):
+    return lax.broadcasted_iota(jnp.int32, shape, dim)
+
+
+def total(mask, values, axis):
+    return jnp.sum(jnp.where(mask, values, 0), axis=axis, keepdims=True)
+
+
+def column(row):
+    n = row.shape[1]
+    return total(iota((n, n), 0) == iota((n, n), 1), row, 1)
+
+
+def ranks(row):
+    n = row.shape[1]
+    key = row * n + iota((1, n), 1)
+    return total(key < column(key), 1, 1)
+
+
+def sort_by(rank, col):
+    n = col.shape[0]
+    return total(rank == iota((n, n), 1), col, 0)
+
+
+def placed(place, row):
+    n = place.shape[0]
+    return total(iota((n, row.shape[1]), 0) == row, place, 0)
 
 
 PARTS = 4
@@ -44,12 +56,13 @@
 
 
 def whole_kernel(
-    g_order, g_src, m_order, m_src, perm, place, halo_at,
+    g_src_h, g_dst_h, m_src_h, m_dst_h, halo_h,
     send_row, grid_latent, latent_in, g_weight, m_weight,
-    a_in_h, a_out_h, e_in_h, e_out_h, e_gain, m_in_h, m_out_h, u_in_h, u_out_h, u_gain,
+    a_in_h, a_out_h, e_in_h, e_out_h, e_gain_h, m_in_h, m_out_h, u_in_h, u_out_h, u_gain_h,
     out_h,
-    grid_x, a_in, a_out, e_in, e_out, m_in, m_out, u_in, u_out, latent,
-    raw, wt_g, wt_m, table, ag0, ag1, ag2, ag3, s0, s1, s2, r0, r1, r2, r3,
+    grid_x, a_in, a_out, e_in, e_out, m_in, m_out, u_in, u_out, e_gain, u_gain, latent,
+    g_from, g_to, m_from, m_to, halo_of, index_v, index_s,
+    lanes_g, lanes_m, raw, wt_g, wt_m, table, ag0, ag1, ag2, ag3, s0, s1, s2, r0, r1, r2, r3,
     state, mine, ptable0, ptable1, payload0, payload1, own_row, rows_v, rows_s,
     chunk_sem, load_sem, row_s, row_r, ag_s, ag_r, relay_s, relay_r, mid_s, mid_r, last_s, last_r, local_sem,
     send_sem, recv_sem,
@@ -57,7 +70,7 @@
     blocks, rows, width = latent.shape
     grid_blocks = grid_x.shape[0]
     sub = rows // PARTS
-    rim = halo_at.shape[0]
+    rim = halo_of.shape[1]
     steps = m_in.shape[0]
     ptable, payload = (ptable0, ptable1), (payload0, payload1)
     ag, stage, held = (ag0, ag1, ag2, ag3), (s0, s1, s2, s0), (r0, r1, r2, r3)
@@ -83,7 +96,9 @@
     loads = [
         pltpu.make_async_copy(src, dst, load_sem.at[i])
         for i, (src, dst) in enumerate((
-            (a_in_h, a_in), (a_out_h, a_out), (send_row, own_row), (g_weight, raw), (latent_in, latent),
+            (a_in_h, a_in), (a_out_h, a_out), (send_row, own_row),
+            (g_src_h, g_from), (g_dst_h, g_to), (m_src_h, m_from), (m_dst_h, m_to), (halo_h, halo_of),
+            (g_weight, lanes_g), (m_weight, lanes_m), (latent_in, latent), (e_gain_h, e_gain), (u_gain_h, u_gain),
             (e_in_h, e_in), (e_out_h, e_out), (m_in_h, m_in), (m_out_h, m_out), (u_in_h, u_in), (u_out_h, u_out),
         ))
     ]
@@ -233,18 +248,63 @@
             last_copy(p, by, flip).start()
         keep_copy(p).start()
 
-    slots_g = g_src.shape[0] // blocks
-    slots_m = m_src.shape[0] // blocks
+    slots_g = g_to.shape[1] // blocks
+    slots_m = m_to.shape[1] // blocks
+    packed = 16
+
+    def listed(r, n=1):
+        return lambda k: index_s[r, k]
+
+    g_order, g_src, m_order, m_src, perm, place, halo_at = [listed(r) for r in range(7)]
+
+    def index_lists():
+        halo_row = halo_of[...]
+        named = iota((blocks, rim), 0) == halo_row
+        first = jnp.min(
+            jnp.where(named, iota((blocks, rim), 1), rim + iota((blocks, rim), 0)), axis=1, keepdims=True)
+        first_row = total(iota((blocks, blocks), 0) == iota((blocks, blocks), 1), first, 0)
+        spot = total(first_row < first, 1, 1)
+        rank_g = ranks(placed(spot, g_to[...]))
+        rank_m = ranks(placed(spot, m_to[...]))
+        m_row = m_from[...]
+        own = jnp.where(m_row < blocks, placed(spot, jnp.minimum(m_row, blocks - 1)), m_row)
+        ng, nm = g_to.shape[1], m_to.shape[1]
+        for r, row in enumerate((
+            sort_by(rank_g, iota((ng, 1), 0)), sort_by(rank_g, column(g_from[...])),
+            sort_by(rank_m, iota((nm, 1), 0)), sort_by(rank_m, column(own)),
+            sort_by(spot, iota((blocks, 1), 0)),
+            total(iota((blocks, blocks), 0) == iota((blocks, blocks), 1), spot, 0),
+            placed(spot, halo_row),
+        )):
+            index_v[pl.ds(r, 1), pl.ds(0, row.shape[1])] = row
+        copy = pltpu.make_async_copy(index_v, index_s, local_sem.at[7])
+        copy.start()
+        return copy
+
+    def unpack(lanes, base, first, last):
+        def body(q, _):
+            x = lanes[pl.ds(q * packed, packed)]
+            tiles = jnp.swapaxes(jnp.swapaxes(x, 1, 2), 0, 1)
+            raw[pl.ds(base, tiles.shape[0]), pl.ds(q * packed, packed)] = tiles
+            return 0
+        lax.fori_loop(first, last, body, 0)
 
     def prepare(order, base, wt, slots):
         def body(b, _):
-            cat = jnp.concatenate([raw[base + order[b * slots + k]] for k in range(slots)], axis=0)
+            cat = jnp.concatenate([raw[base + order(b * slots + k)] for k in range(slots)], axis=0)
             wt[b] = cat.T
             return 0
         lax.fori_loop(0, blocks, body, 0)
 
+    groups = rows // packed
+    for c in loads[3:8]:
+        c.wait()
+    lists = index_lists()
+    loads[8].wait()
+    unpack(lanes_g, 0, 0, 2)
     for p in range(3):
         relays(p)
+    unpack(lanes_g, 0, 2, groups)
     for a in range(3):
         own_rows[a].wait()
         for by in (1, 2, 3):
@@ -252,6 +312,7 @@
     to_scalar = pltpu.make_async_copy(rows_v, rows_s, local_sem.at[0])
     to_scalar.start()
     to_scalar.wait()
+    lists.wait()
 
     gathered(0)
     for h in (0, 1):
@@ -261,28 +322,28 @@
     gathered(1)
     select(1)
     gathered(2)
-    loads[3].wait()
     prepare(g_order, 0, wt_g, slots_g)
-    m_load = pltpu.make_async_copy(m_weight, raw, load_sem.at[3])
-    m_load.start()
     relays(3)
+    loads[9].wait()
+    half_tiles = raw.shape[0] // steps
+    unpack(lanes_m.at[0], 0, 0, groups)
     gathered(3)
     select(2)
+    unpack(lanes_m.at[1], half_tiles, 0, groups)
     arrived(0)
     for by in (1, 2, 3):
         mid_copy(0, by).wait_send()
     select(3)
     deliver(0)
-    m_load.wait()
     for s in range(steps):
-        prepare(m_order, s * (raw.shape[0] // steps), wt_m.at[s], slots_m)
+        prepare(m_order, s * half_tiles, wt_m.at[s], slots_m)
     arrived(1)
     arrived(2)
     deliver(1)
     deliver(2)
     arrived(3)
     deliver(3)
-    for c in loads[4:]:
+    for c in loads[10:]:
         c.wait()
     for p in range(PARTS):
         for by, flip in others:
@@ -311,7 +372,7 @@
         parts = []
         for i in range(quarter):
             p = c * quarter + i
-            got = jnp.concatenate([load(idx[p * slots + k]) for k in range(slots)], axis=0)
+            got = jnp.concatenate([load(idx(p * slots + k)) for k in range(slots)], axis=0)
             parts.append(mm(wt[p], got).astype(BF16))
         return jnp.concatenate(parts, axis=0)
 
@@ -333,13 +394,13 @@
 
     def push(s, h):
         for i in range(half_rim):
-            payload[s][h * half_rim + i] = mine[halo_at[h * half_rim + i]]
+            payload[s][h * half_rim + i] = mine[halo_at(h * half_rim + i)]
         for c in halo(s, h):
             c.start()
 
     def enc_chunk(c):
         agg = summed(from_grid, g_src, wt_g, slots_g, c)
-        old = jnp.concatenate([latent[perm[c * quarter + i]] for i in range(quarter)], axis=0)
+        old = jnp.concatenate([latent[perm(c * quarter + i)] for i in range(quarter)], axis=0)
         new = update(old, agg, e_in, e_out, e_gain[...])
         state[pl.ds(c * quarter, quarter)] = new.reshape(quarter, rows, width)
         message(0, c, new)
@@ -377,7 +438,7 @@
             rest(functools.partial(proc_chunk, s), 0)
 
     def restore(b, _):
-        mine[b] = state[place[b]]
+        mine[b] = state[place(b)]
         return 0
 
     lax.fori_loop(0, blocks, restore, 0)
@@ -408,23 +469,8 @@
     steps = proc_msg_in.shape[0]
     rim = halo_send.shape[1]
     peers = g2m_send.shape[1]
-    vmem = pl.BlockSpec(memory_space=pltpu.VMEM)
-    smem = pl.BlockSpec(memory_space=pltpu.SMEM)
     hbm = pl.BlockSpec(memory_space=pl.ANY)
 
-    ids = jnp.arange(blocks, dtype=jnp.int32)
-    named = halo_send[0][None, :] == ids[:, None]
-    first = jnp.min(
-        jnp.where(named, jnp.arange(rim, dtype=jnp.int32)[None, :], rim + ids[:, None]), axis=1
-    )
-    place = jnp.sum((first[None, :] < first[:, None]).astype(jnp.int32), axis=1)
-    perm = invert(place)
-    halo_at = pick(place, halo_send[0])
-    g_order = grouped(pick(place, g2m_dst[0]))
-    m_order = grouped(pick(place, m2m_dst[0]))
-    g_src = pick(g2m_src[0], g_order)
-    m_from = pick(m2m_src[0], m_order)
-    m_src = jnp.where(m_from < blocks, pick(place, m_from), m_from)
     sub = rows // PARTS
     flying = (4, grid_blocks, sub, width)
     staged = (3, 4, 4, 2, sub, width)
@@ -434,14 +480,21 @@
     out = pl.pallas_call(
         whole_kernel,
         out_shape=jax.ShapeDtypeStruct((blocks, rows, width), BF16),
-        in_specs=[smem] * 7 + [hbm] * 9 + [vmem] + [hbm] * 4 + [vmem],
+        in_specs=[hbm] * 20,
         out_specs=hbm,
         scratch_shapes=[
             vm((grid_blocks, rows, width), BF16),
             *[vm(w.shape, BF16) for w in (
                 enc_msg_in, enc_msg_out, enc_upd_in, enc_upd_out,
                 proc_msg_in, proc_msg_out, proc_upd_in, proc_upd_out)],
+            vm((1, width), F32),
+            vm((steps, width), F32),
             vm((blocks, rows, width), BF16),
+            *[vm(v.shape, jnp.int32) for v in (g2m_src, g2m_dst, m2m_src, m2m_dst, halo_send)],
+            vm((8, 256), jnp.int32),
+            pltpu.SMEM((8, 256), jnp.int32),
+            vm((rows, rows, g2m_dst.shape[1]), BF16),
+            vm((steps, rows, rows, m2m_dst.shape[1]), BF16),
             vm(g2m_weight.shape, BF16),
             vm((blocks, rows, rows * (g2m_dst.shape[1] // blocks)), BF16),
             vm((steps, blocks, rows, rows * (m2m_dst.shape[1] // blocks)), BF16),
@@ -458,9 +511,9 @@
             vm((1, peers), jnp.int32),
             vm((3, 4, 1, peers), jnp.int32),
             pltpu.SMEM((3, 4, 1, peers), jnp.int32),
-            dma((8,)), dma((11,)), dma((3, 3)), dma((3, 3)),
+            dma((8,)), dma((19,)), dma((3, 3)), dma((3, 3)),
             dma((4, 2, 2)), dma((4, 2, 2)), dma((4, 2)), dma((4, 2)),
-            dma((4, 3)), dma((4, 3)), dma((4, 4, 2)), dma((4, 4, 2)), dma((7,)),
+            dma((4, 3)), dma((4, 3)), dma((4, 4, 2)), dma((4, 4, 2)), dma((8,)),
             dma((steps, 2, 2)), dma((steps, 2, 2)),
         ],
         compiler_params=pltpu.CompilerParams(
@@ -468,9 +521,9 @@
         ),
         name="encoder_and_steps",
     )(
-        g_order, g_src, m_order, m_src, perm, place, halo_at,
+        g2m_src, g2m_dst, m2m_src, m2m_dst, halo_send,
         g2m_send, grid_latent.reshape(grid_blocks, rows, width), mesh_latent.reshape(blocks, rows, width),
-        g2m_weight, m2m_weight.reshape(g2m_weight.shape),
+        jnp.transpose(g2m_weight, (1, 2, 0)), jnp.transpose(m2m_weight, (0, 2, 3, 1)),
         enc_msg_in, enc_msg_out, enc_upd_in, enc_upd_out, enc_gain.reshape(1, width),
         proc_msg_in, proc_msg_out, proc_upd_in, proc_upd_out, proc_gain,
     )

time: 161 us -> 142 us (0.88)
  local copies, waits for them, and re-layouts: 14 us -> 2.26 us
  other arithmetic: 7.94 us -> 0 us
    unnamed x11 -> x1, local copies, waits for them, and re-layouts: 14 us -> 2.26 us
    reduce_sum x12 -> x0, other arithmetic: 6.65 us -> none  [the longest x6 5.24 us: pick(): return jnp.sum(jnp.where(hit, table[None, :], 0), axis=1)]
where the time goes in v3:
time: 142 us; the launch traced here: 140 us
  Pallas kernels  137 us (96%)
  local copies, waits for them, and re-layouts  2.26 us (2%)
    pallas_call x1, Pallas kernels, on_device(): pl.pallas_call(whole_kernel, out_shape=jax.ShapeDtypeStruct((blocks, rows...  137 us

profile of v3, /device:TPU:1, one launch (start us, length us, event | category | flops | bytes accessed | tf_op | source)
XLA Modules:
  0.0 139.6 jit_solution(16110851638963209325)
XLA Ops:
  0.0 137.3 %encoder_and_steps.1 = bf16[16,64,512]{2,1,0:T(8,128)(2,1)} custom-call(s32[1,224]{1,0:T(1,128)} %g_src_h.1, s32[1,224]{1,0:T(1,128)} %g_dst_h.1, s32[1,112]{1,0:T(1,128)} %m_src_h.1, s32[1,112]{1,0:T(1,128)} %m_dst_h.1, s32[1,8]{1,0:T(1,128)} %halo_h.1, s32[1,128]{1,0:T(1,128)} %send_row.1, bf16[32,64,512]{2,1,0:T(8,128)(2,1)} %bitcast.7, ...), custom_call_target="tpu_custom_call" | custom-call | tf_op jit(solution)/shard_map/encoder_and_steps/pallas_call | solution.py:480
  137.4 2.3 %copy.22 = bf16[1024,512]{1,0:T(8,128)(2,1)} copy(bf16[1024,512]{1,0:T(8,128)(2,1)} %bitcast.6) | data formatting | bytes 2097152

commit v4 on v3

--- a/solution.py
+++ b/solution.py
@@ -50,6 +50,14 @@
     return total(iota((n, row.shape[1]), 0) == row, place, 0)
 
 
+def loop(first, last, step):
+    def body(i, _):
+        step(i)
+        return 0
+
+    lax.fori_loop(first, last, body, 0)
+
+
 PARTS = 4
 LINES = (("x", "y", "z"), ("y", "z", "x"), ("z", "x", "y"), ("x", "y", "z"))
 AXES = ("x", "y", "z")
@@ -60,20 +68,23 @@
     send_row, grid_latent, latent_in, g_weight, m_weight,
     a_in_h, a_out_h, e_in_h, e_out_h, e_gain_h, m_in_h, m_out_h, u_in_h, u_out_h, u_gain_h,
     out_h,
-    grid_x, a_in, a_out, e_in, e_out, m_in, m_out, u_in, u_out, e_gain, u_gain, latent,
+    a_in, a_out, e_in, e_out, m_in, m_out, u_in, u_out, e_gain, u_gain, latent,
     g_from, g_to, m_from, m_to, halo_of, index_v, index_s,
-    lanes_g, lanes_m, raw, wt_g, wt_m, table, ag0, ag1, ag2, ag3, s0, s1, s2, r0, r1, r2, r3,
+    lanes_g, lanes_m, raw, wt_g, wt_m, table,
+    a00, a01, a02, a03, a10, a11, a12, a13, a20, a21, a22, a23, a30, a31, a32, a33,
+    s0, s1, s2, s3, r0, r1, r2, r3,
     state, mine, ptable0, ptable1, payload0, payload1, own_row, rows_v, rows_s,
-    chunk_sem, load_sem, row_s, row_r, ag_s, ag_r, relay_s, relay_r, mid_s, mid_r, last_s, last_r, local_sem,
+    chunk_sem, load_sem, row_s, row_r, ag_s, ag_r, relay_s, relay_r, mid_s, mid_r, last_s, last_r, keep_sem, local_sem,
     send_sem, recv_sem,
 ):
     blocks, rows, width = latent.shape
-    grid_blocks = grid_x.shape[0]
+    grid_blocks = grid_latent.shape[0]
     sub = rows // PARTS
     rim = halo_of.shape[1]
     steps = m_in.shape[0]
     ptable, payload = (ptable0, ptable1), (payload0, payload1)
-    ag, stage, held = (ag0, ag1, ag2, ag3), (s0, s1, s2, s0), (r0, r1, r2, r3)
+    ag = ((a00, a01, a02, a03), (a10, a11, a12, a13), (a20, a21, a22, a23), (a30, a31, a32, a33))
+    stage, held = (s0, s1, s2, s3), (r0, r1, r2, r3)
     tile = lax.axis_index("tile")
     core = lax.rem(tile, 2)
     at = {"x": lax.axis_index("dom"), "y": lax.rem(tile // 2, 4), "z": tile // 8}
@@ -89,9 +100,10 @@
     chunk = 4
     chunks = grid_blocks // chunk
 
-    def chunk_load(i):
+    def chunk_load(h, i):
+        n = h * (chunks // 2) + i
         return pltpu.make_async_copy(
-            grid_latent.at[pl.ds(i * chunk, chunk)], grid_x.at[pl.ds(i * chunk, chunk)], chunk_sem.at[i])
+            grid_latent.at[pl.ds(n * chunk, chunk)], (state, mine)[h].at[pl.ds(i * chunk, chunk)], chunk_sem.at[n])
 
     loads = [
         pltpu.make_async_copy(src, dst, load_sem.at[i])
@@ -103,45 +115,40 @@
         ))
     ]
     loads[0].start()
-    chunk_load(0).start()
+    chunk_load(0, 0).start()
     loads[1].start()
     loads[2].start()
     for i in range(1, chunks):
-        chunk_load(i).start()
-    for c in loads[3:]:
-        c.start()
+        chunk_load(i // (chunks // 2), i % (chunks // 2)).start()
 
     barrier = pltpu.get_barrier_semaphore()
     greeted = [moved(axis, by, flip) for axis in AXES for by in (1, 2, 3) for flip in (0, 1)] + [moved("x", 0, 1)]
     for peer in greeted:
         pl.semaphore_signal(barrier, inc=1, device_id=peer, device_id_type=MESH)
 
-    def mlp(i, _):
-        chunk_load(i).wait()
-        x = grid_x[pl.ds(i * chunk, chunk)].reshape(chunk * rows, width)
-        h = silu(mm(x, a_in[...])).astype(BF16)
-        msg = mm(h, a_out[...]).astype(BF16).reshape(chunk, rows, width)
+    def mlp(h, k):
+        chunk_load(h, k).wait()
+        i = h * (chunks // 2) + k
+        x = (state, mine)[h][pl.ds(k * chunk, chunk)].reshape(chunk * rows, width)
+        hidden = silu(mm(x, a_in[...])).astype(BF16)
+        msg = mm(hidden, a_out[...]).astype(BF16).reshape(chunk, rows, width)
         table[0, i // 2, lax.rem(i, 2)] = msg
         for p in range(PARTS):
-            ag[p][at[LINES[p][0]], pl.ds(i * chunk, chunk)] = msg[:, p * sub:(p + 1) * sub]
-        return 0
+            ag[p][0][pl.ds(i * chunk, chunk)] = msg[:, p * sub:(p + 1) * sub]
 
     half = grid_blocks // 2
 
     def gather_copy(p, way, h):
-        axis = LINES[p][0]
-        ref = ag[p].at[at[axis], pl.ds(h * half, half)]
+        here = pl.ds(h * half, half)
         return pltpu.make_async_remote_copy(
-            ref, ref, ag_s.at[p, way, h], ag_r.at[p, way, h],
-            device_id=moved(axis, 1 - 2 * way), device_id_type=MESH)
+            ag[p][0].at[here], ag[p][3 - 2 * way].at[here], ag_s.at[p, way, h], ag_r.at[p, way, h],
+            device_id=moved(LINES[p][0], 1 - 2 * way), device_id_type=MESH)
 
     def relay_copy(p, way):
-        axis = LINES[p][0]
-        by = 1 - 2 * way
-        ref = ag[p].at[lax.rem(at[axis] - by + 4, 4), pl.ds(way * half, half)]
+        here = pl.ds(way * half, half)
         return pltpu.make_async_remote_copy(
-            ref, ref, relay_s.at[p, way], relay_r.at[p, way],
-            device_id=moved(axis, by), device_id_type=MESH)
+            ag[p][3 - 2 * way].at[here], ag[p][2].at[here], relay_s.at[p, way], relay_r.at[p, way],
+            device_id=moved(LINES[p][0], 1 - 2 * way), device_id_type=MESH)
 
     def row_copy(a, by):
         axis = AXES[a]
@@ -151,7 +158,7 @@
 
     loads[0].wait()
     loads[1].wait()
-    lax.fori_loop(0, chunks // 2, mlp, 0)
+    loop(0, chunks // 2, functools.partial(mlp, 0))
     pl.semaphore_wait(barrier, len(greeted))
     for p in range(3):
         for way in (0, 1):
@@ -163,96 +170,112 @@
     own_rows = [pltpu.make_async_copy(own_row, rows_v.at[a, at[AXES[a]]], local_sem.at[a]) for a in range(3)]
     for c in own_rows:
         c.start()
-    lax.fori_loop(chunks // 2, chunks, mlp, 0)
+    loop(0, chunks // 2, functools.partial(mlp, 1))
     for p in range(3):
         for way in (0, 1):
             gather_copy(p, way, 1).start()
+
+    for c in loads[3:]:
+        c.start()
 
     def relays(p):
         for way in (0, 1):
             gather_copy(p, way, way).wait_recv()
             relay_copy(p, way).start()
 
-    def gathered(p):
+    def near(p):
         for way in (0, 1):
             gather_copy(p, way, 1 - way).wait_recv()
+
+    def far(p):
+        for way in (0, 1):
             relay_copy(p, way).wait_recv()
 
-    def held_at(p, b):
-        return held[p].at[:, b] if p == 2 else held[p].at[b]
-
-    def mid_copy(p, by):
-        axis = LINES[p][1]
+    def spread(p):
+        for h in (0, 1):
+            for way in (0, 1):
+                gather_copy(p, way, h).start()
+
+    def held_at(p, b, j):
+        return (j, b) if p == 2 else (b, j)
+
+    def mid_copy(p, by, j):
+        first, second, _ = LINES[p]
+        b, k = held_at(p, at[second], lax.rem(at[first] + j, 4))
         return pltpu.make_async_remote_copy(
-            stage[p].at[by - 1], held_at(p, at[axis]), mid_s.at[p, by - 1], mid_r.at[p, by - 1],
-            device_id=moved(axis, by), device_id_type=MESH)
-
-    def select(p):
+            stage[p].at[by - 1, j], held[p].at[b, k], mid_s.at[p, by - 1, j], mid_r.at[p, by - 1, j],
+            device_id=moved(second, by), device_id_type=MESH)
+
+    def select(p, js):
         first, second, third = LINES[p]
         a = AXES.index(first)
 
         def of(by, j):
             c = dict(at)
             c[second] = lax.rem(at[second] + by, 4)
+            row = lax.rem(at[first] + j, 4)
             for k in range(8):
                 c[third] = k // 2
                 t, x = device(c, k % 2)
-                got = ag[p][j, rows_s[a, j, 0, t * 4 + x]]
-                yield k // 2, k % 2, got
-
-        def keep(j, _):
+                yield k // 2, k % 2, ag[p][j][rows_s[a, row, 0, t * 4 + x]]
+
+        for j in js:
+            def put(by, _):
+                for c3, k, got in of(by, j):
+                    stage[p][by - 1, j, c3, k] = got
+                return 0
+
+            lax.fori_loop(1, 4, put, 0)
+            b, row = held_at(p, at[second], lax.rem(at[first] + j, 4))
             for c3, k, got in of(0, j):
-                if p == 2:
-                    held[p][j, at[second], c3, k] = got
-                else:
-                    held[p][at[second], j, c3, k] = got
-            return 0
-
-        def put(i, _):
-            by, j = 1 + i // 4, lax.rem(i, 4)
-            for c3, k, got in of(by, j):
-                stage[p][by - 1, j, c3, k] = got
-            return 0
-
-        lax.fori_loop(0, 12, put, 0)
-        for by in (1, 2, 3):
-            mid_copy(p, by).start()
-        lax.fori_loop(0, 4, keep, 0)
-
-    def arrived(p):
-        for by in (1, 2, 3):
-            mid_copy(p, by).wait_recv()
-
-    def landing(p):
+                held[p][b, row, c3, k] = got
+
+    def pass_on(p, js):
+        for j in js:
+            for by in (1, 3, 2):
+                mid_copy(p, by, j).start()
+
+    def arrived(p, js):
+        for j in js:
+            loop(1, 4, lambda by: mid_copy(p, by, j).wait_recv())
+
+    def landing(p, b):
         here = pl.ds(p * sub, sub)
         if p == 1:
-            return table.at[pl.ds(1, 4), :, core, at["x"], here]
+            return table.at[1 + b, :, core, at["x"], here]
         if p == 2:
-            return table.at[pl.ds(1, 4), at["y"], core, :, here]
-        return table.at[1 + at["z"], :, core, :, here]
-
-    others = [(by, flip) for by in (1, 3, 2, 0) for flip in (0, 1) if by or flip]
-
-    def last_copy(p, by, flip):
-        axis = LINES[p][2]
+            return table.at[pl.ds(1, 4), at["y"], core, b, here]
+        return table.at[1 + at["z"], b, core, :, here]
+
+    def leaving(p, b, c3, k):
+        return held[p].at[:, b, c3, k] if p == 2 else held[p].at[b, :, c3, k]
+
+    def last_copy(p, bi, k):
+        _, second, axis = LINES[p]
+        by, flip = k // 2, lax.rem(k, 2)
+        b = lax.rem(at[second] + bi, 4)
         return pltpu.make_async_remote_copy(
-            held[p].at[:, :, lax.rem(at[axis] + by, 4), lax.rem(core + flip, 2)], landing(p),
-            last_s.at[p, by, flip], last_r.at[p, by, flip],
+            leaving(p, b, lax.rem(at[axis] + by, 4), lax.rem(core + flip, 2)), landing(p, b),
+            last_s.at[p, bi, k], last_r.at[p, bi, k],
             device_id=moved(axis, by, flip), device_id_type=MESH)
 
-    def keep_copy(p):
-        return pltpu.make_async_copy(held[p].at[:, :, at[LINES[p][2]], core], landing(p), local_sem.at[3 + p])
-
-    def deliver(p):
-        for by, flip in others:
-            last_copy(p, by, flip).start()
-        keep_copy(p).start()
+    def keep_copy(p, bi):
+        _, second, axis = LINES[p]
+        b = lax.rem(at[second] + bi, 4)
+        return pltpu.make_async_copy(leaving(p, b, at[axis], core), landing(p, b), keep_sem.at[p, bi])
+
+    def deliver(p, first, last):
+        def one(bi):
+            loop(1, 8, lambda k: last_copy(p, bi, k).start())
+            keep_copy(p, bi).start()
+
+        loop(first, last, one)
 
     slots_g = g_to.shape[1] // blocks
     slots_m = m_to.shape[1] // blocks
     packed = 16
 
-    def listed(r, n=1):
+    def listed(r):
         return lambda k: index_s[r, k]
 
     g_order, g_src, m_order, m_src, perm, place, halo_at = [listed(r) for r in range(7)]
@@ -314,41 +337,61 @@
     to_scalar.wait()
     lists.wait()
 
-    gathered(0)
-    for h in (0, 1):
-        for way in (0, 1):
-            gather_copy(3, way, h).start()
-    select(0)
-    gathered(1)
-    select(1)
-    gathered(2)
+    every, close = (0, 1, 3, 2), (0, 1, 3)
+    select(0, (0,))
+    select(1, (0,))
+    near(0)
+    spread(3)
+    select(0, (1, 3))
+    pass_on(0, close)
+    near(1)
+    select(1, (1, 3))
+    pass_on(1, close)
+    near(2)
+    select(2, close)
+    far(0)
+    select(0, (2,))
+    pass_on(0, (2,))
+    far(1)
+    select(1, (2,))
+    pass_on(1, (2,))
     prepare(g_order, 0, wt_g, slots_g)
+    far(2)
+    select(2, (2,))
     relays(3)
     loads[9].wait()
     half_tiles = raw.shape[0] // steps
-    unpack(lanes_m.at[0], 0, 0, groups)
-    gathered(3)
-    select(2)
+    unpack(lanes_m.at[0], 0, 0, 2)
+    select(3, (0,))
+    near(3)
+    pass_on(2, every)
+    select(3, (1, 3))
+    deliver(0, 0, 1)
+    far(3)
+    select(3, (2,))
+    pass_on(3, every)
+    unpack(lanes_m.at[0], 0, 2, groups)
+    arrived(0, every)
+    deliver(0, 1, 4)
     unpack(lanes_m.at[1], half_tiles, 0, groups)
-    arrived(0)
-    for by in (1, 2, 3):
-        mid_copy(0, by).wait_send()
-    select(3)
-    deliver(0)
     for s in range(steps):
         prepare(m_order, s * half_tiles, wt_m.at[s], slots_m)
-    arrived(1)
-    arrived(2)
-    deliver(1)
-    deliver(2)
-    arrived(3)
-    deliver(3)
+    arrived(1, every)
+    arrived(2, close)
+    deliver(1, 0, 4)
+    deliver(3, 0, 1)
+    arrived(2, (2,))
+    deliver(2, 0, 4)
+    arrived(3, every)
+    deliver(3, 1, 4)
     for c in loads[10:]:
         c.wait()
     for p in range(PARTS):
-        for by, flip in others:
-            last_copy(p, by, flip).wait_recv()
-        keep_copy(p).wait()
+        def landed(bi):
+            loop(1, 8, lambda k: last_copy(p, bi, k).wait_recv())
+            keep_copy(p, bi).wait()
+
+        loop(0, 4, landed)
 
     n_dom = lax.axis_size("dom")
     upper, lower = moved("x", 1), moved("x", 3)
@@ -449,11 +492,11 @@
             relay_copy(p, way).wait_send()
             for h in (0, 1):
                 gather_copy(p, way, h).wait_send()
-        for by, flip in others:
-            last_copy(p, by, flip).wait_send()
-        if p:
-            for by in (1, 2, 3):
-                mid_copy(p, by).wait_send()
+        def sent(j):
+            loop(1, 4, lambda by: mid_copy(p, by, j).wait_send())
+            loop(1, 8, lambda k: last_copy(p, j, k).wait_send())
+
+        loop(0, 4, sent)
     store.wait()
 
 
@@ -472,7 +515,7 @@
     hbm = pl.BlockSpec(memory_space=pl.ANY)
 
     sub = rows // PARTS
-    flying = (4, grid_blocks, sub, width)
+    flying = (grid_blocks, sub, width)
     staged = (3, 4, 4, 2, sub, width)
     holding = (4, 4, 4, 2, sub, width)
     dma = pltpu.SemaphoreType.DMA
@@ -483,7 +526,6 @@
         in_specs=[hbm] * 20,
         out_specs=hbm,
         scratch_shapes=[
-            vm((grid_blocks, rows, width), BF16),
             *[vm(w.shape, BF16) for w in (
                 enc_msg_in, enc_msg_out, enc_upd_in, enc_upd_out,
                 proc_msg_in, proc_msg_out, proc_upd_in, proc_upd_out)],
@@ -499,8 +541,8 @@
             vm((blocks, rows, rows * (g2m_dst.shape[1] // blocks)), BF16),
             vm((steps, blocks, rows, rows * (m2m_dst.shape[1] // blocks)), BF16),
             vm((5, 4, 2, 4, rows, width), BF16),
-            *[vm(flying, BF16)] * 4,
-            *[vm(staged, BF16)] * 3,
+            *[vm(flying, BF16)] * 16,
+            *[vm(staged, BF16)] * 4,
             *[vm(holding, BF16)] * 4,
             vm((blocks, rows, width), BF16),
             vm((blocks, rows, width), BF16),
@@ -513,7 +555,7 @@
             pltpu.SMEM((3, 4, 1, peers), jnp.int32),
             dma((8,)), dma((19,)), dma((3, 3)), dma((3, 3)),
             dma((4, 2, 2)), dma((4, 2, 2)), dma((4, 2)), dma((4, 2)),
-            dma((4, 3)), dma((4, 3)), dma((4, 4, 2)), dma((4, 4, 2)), dma((8,)),
+            dma((4, 3, 4)), dma((4, 3, 4)), dma((4, 4, 8)), dma((4, 4, 8)), dma((4, 4)), dma((8,)),
             dma((steps, 2, 2)), dma((steps, 2, 2)),
         ],
         compiler_params=pltpu.CompilerParams(

time: 142 us -> 140 us (0.986); the launches traced: 140 us -> 140 us
  no operation moved by 1% of the time
where the time goes in v4:
time: 140 us
  Pallas kernels  138 us (99%)
  local copies, waits for them, and re-layouts  2.26 us (2%)
    pallas_call x1, Pallas kernels, on_device(): pl.pallas_call(whole_kernel, out_shape=jax.ShapeDtypeStruct((blocks, rows...  138 us

profile of v4, /device:TPU:1, one launch (start us, length us, event | category | flops | bytes accessed | tf_op | source)
XLA Modules:
  0.0 140.0 jit_solution(10326112622718078337)
XLA Ops:
  0.0 137.7 %encoder_and_steps.1 = bf16[16,64,512]{2,1,0:T(8,128)(2,1)} custom-call(s32[1,224]{1,0:T(1,128)} %g_src_h.1, s32[1,224]{1,0:T(1,128)} %g_dst_h.1, s32[1,112]{1,0:T(1,128)} %m_src_h.1, s32[1,112]{1,0:T(1,128)} %m_dst_h.1, s32[1,8]{1,0:T(1,128)} %halo_h.1, s32[1,128]{1,0:T(1,128)} %send_row.1, bf16[32,64,512]{2,1,0:T(8,128)(2,1)} %bitcast.7, ...), custom_call_target="tpu_custom_call" | custom-call | tf_op jit(solution)/shard_map/encoder_and_steps/pallas_call | solution.py:523
  137.7 2.3 %copy.22 = bf16[1024,512]{1,0:T(8,128)(2,1)} copy(bf16[1024,512]{1,0:T(8,128)(2,1)} %bitcast.6) | data formatting | bytes 2097152

commit v5 on v4

--- a/solution.py
+++ b/solution.py
@@ -196,6 +196,12 @@
             for way in (0, 1):
                 gather_copy(p, way, h).start()
 
+    def spread_out(p):
+        for way in (0, 1):
+            relay_copy(p, way).wait_send()
+            for h in (0, 1):
+                gather_copy(p, way, h).wait_send()
+
     def held_at(p, b, j):
         return (j, b) if p == 2 else (b, j)
 
@@ -318,6 +324,28 @@
             wt[b] = cat.T
             return 0
         lax.fori_loop(0, blocks, body, 0)
+
+    def rim_weights(s, base, h):
+        side = iota((rows, 2 * rows), 1) // rows
+        wide = 2 * rows
+
+        def one(n):
+            b = h * (blocks // 2) + n
+            src = [m_src(b * slots_m + k) for k in range(slots_m)]
+            tiles = [raw[base + m_order(b * slots_m + k)] for k in range(slots_m)]
+            own = [jnp.where(src[k] < blocks, tiles[k], jnp.zeros_like(tiles[k])) for k in range(slots_m)]
+            wt_m[s, b] = jnp.concatenate(own, axis=0).T
+            twice = jnp.concatenate([t for t in tiles for _ in (0, 1)], axis=0).T.astype(F32)
+            for pair in range(rim):
+                acc = jnp.zeros((rows, wide), F32)
+                for k in range(slots_m):
+                    hit = side + (blocks + 2 * pair) == src[k]
+                    acc = acc + jnp.where(hit, twice[:, k * wide:(k + 1) * wide], 0.0)
+                q, lane = pair // (rim // 2), pair % (rim // 2)
+                ag[s][2 * q + h][pl.ds(n * PARTS, PARTS), :, pl.ds(lane * wide, wide)] = (
+                    acc.astype(BF16).reshape(PARTS, sub, wide))
+
+        loop(0, blocks // 2, one)
 
     groups = rows // packed
     for c in loads[3:8]:
@@ -361,25 +389,28 @@
     relays(3)
     loads[9].wait()
     half_tiles = raw.shape[0] // steps
-    unpack(lanes_m.at[0], 0, 0, 2)
+    unpack(lanes_m.at[0], 0, 0, groups)
     select(3, (0,))
     near(3)
     pass_on(2, every)
     select(3, (1, 3))
     deliver(0, 0, 1)
+    unpack(lanes_m.at[1], half_tiles, 0, groups)
     far(3)
     select(3, (2,))
     pass_on(3, every)
-    unpack(lanes_m.at[0], 0, 2, groups)
+    for p in range(2):
+        spread_out(p)
+    rim_weights(0, 0, 0)
     arrived(0, every)
     deliver(0, 1, 4)
-    unpack(lanes_m.at[1], half_tiles, 0, groups)
-    for s in range(steps):
-        prepare(m_order, s * half_tiles, wt_m.at[s], slots_m)
+    rim_weights(0, 0, 1)
+    rim_weights(1, half_tiles, 0)
     arrived(1, every)
     arrived(2, close)
     deliver(1, 0, 4)
     deliver(3, 0, 1)
+    rim_weights(1, half_tiles, 1)
     arrived(2, (2,))
     deliver(2, 0, 4)
     arrived(3, every)
@@ -401,23 +432,41 @@
     def halo(s, h):
         src = payload[s].at[pl.ds(h * half_rim, half_rim)]
         up = pltpu.make_async_remote_copy(
-            src, ptable[s].at[pl.ds(blocks + h * half_rim, half_rim)],
+            src, ptable[s].at[pl.ds(h * half_rim, half_rim)],
             send_sem.at[s, 0, h], recv_sem.at[s, 0, h], device_id=upper, device_id_type=MESH)
         down = pltpu.make_async_remote_copy(
-            src, ptable[s].at[pl.ds(blocks + rim + h * half_rim, half_rim)],
+            src, ptable[s].at[pl.ds(rim + h * half_rim, half_rim)],
             send_sem.at[s, 1, h], recv_sem.at[s, 1, h], device_id=lower, device_id_type=MESH)
         return up, down
 
     def from_grid(i):
         return table[i // 32, lax.rem(i // 8, 4), lax.rem(i // 4, 2), lax.rem(i, 4)]
 
-    def summed(load, idx, wt, slots, c):
-        parts = []
-        for i in range(quarter):
-            p = c * quarter + i
-            got = jnp.concatenate([load(idx(p * slots + k)) for k in range(slots)], axis=0)
-            parts.append(mm(wt[p], got).astype(BF16))
-        return jnp.concatenate(parts, axis=0)
+    def tiles_sum(load, idx, wt, slots, p):
+        got = jnp.concatenate([load(idx(p * slots + k)) for k in range(slots)], axis=0)
+        return mm(wt[p], got)
+
+    def own_part(s):
+        def one(p):
+            acc = tiles_sum(lambda i: mine[jnp.minimum(i, blocks - 1)], m_src, wt_m.at[s], slots_m, p)
+            high = acc.astype(BF16)
+            at_p = p // 8, lax.rem(p // 4, 2), lax.rem(p, 4)
+            table[(0, *at_p)] = high
+            table[(1, *at_p)] = (acc - high.astype(F32)).astype(BF16)
+
+        loop(0, blocks, one)
+
+    def rim_part(s, h, k):
+        c = 2 * h + k
+        some = pl.ds(k * quarter * PARTS, quarter * PARTS)
+        acc = jnp.zeros((quarter * rows, width), F32)
+        for q in (0, 1):
+            dense = ag[s][2 * q + h][some].reshape(quarter * rows, rim * rows)
+            acc = acc + mm(dense, ptable[s][pl.ds(q * rim, rim)].reshape(rim * rows, width))
+        at_c = c // 2, lax.rem(c, 2)
+        for level in (0, 1):
+            acc = acc + table[(level, *at_c)].reshape(quarter * rows, width).astype(F32)
+        return acc.astype(BF16)
 
     def update(old, agg, w_in, w_out, gain):
         pre = mm(old, w_in[pl.ds(0, width), :]) + mm(agg, w_in[pl.ds(width, width), :])
@@ -431,9 +480,7 @@
     def message(s, c, new):
         h = silu(mm(new, m_in[s])).astype(BF16)
         msg = mm(h, m_out[s]).astype(BF16)
-        msg = msg.reshape(quarter, rows, width)
-        mine[pl.ds(c * quarter, quarter)] = msg
-        ptable[s][pl.ds(c * quarter, quarter)] = msg
+        mine[pl.ds(c * quarter, quarter)] = msg.reshape(quarter, rows, width)
 
     def push(s, h):
         for i in range(half_rim):
@@ -442,43 +489,39 @@
             c.start()
 
     def enc_chunk(c):
-        agg = summed(from_grid, g_src, wt_g, slots_g, c)
+        agg = jnp.concatenate([
+            tiles_sum(from_grid, g_src, wt_g, slots_g, c * quarter + i).astype(BF16) for i in range(quarter)], axis=0)
         old = jnp.concatenate([latent[perm(c * quarter + i)] for i in range(quarter)], axis=0)
         new = update(old, agg, e_in, e_out, e_gain[...])
         state[pl.ds(c * quarter, quarter)] = new.reshape(quarter, rows, width)
         message(0, c, new)
 
-    def proc_chunk(s, c):
-        agg = summed(lambda i: ptable[s][i], m_src, wt_m.at[s], slots_m, c)
+    def proc_chunk(s, h, k):
+        c = 2 * h + k
         old = state[pl.ds(c * quarter, quarter)].reshape(quarter * rows, width)
-        new = update(old, agg, u_in.at[s], u_out.at[s], u_gain[pl.ds(s, 1), :])
+        new = update(old, rim_part(s, h, k), u_in.at[s], u_out.at[s], u_gain[pl.ds(s, 1), :])
         state[pl.ds(c * quarter, quarter)] = new.reshape(quarter, rows, width)
         if s + 1 < steps:
             message(s + 1, c, new)
-
-    def rest(chunk, first):
-        def body(c, _):
-            chunk(c)
-            return 0
-        lax.fori_loop(first, 4, body, 0)
 
     enc_chunk(0)
     push(0, 0)
     enc_chunk(1)
     push(0, 1)
-    rest(enc_chunk, 2)
+    loop(2, 4, enc_chunk)
     for s in range(steps):
+        own_part(s)
         for h in range(2):
             for c in halo(s, h):
                 c.wait()
         if s + 1 < steps:
-            proc_chunk(s, 0)
+            proc_chunk(s, 0, 0)
             push(s + 1, 0)
-            proc_chunk(s, 1)
+            proc_chunk(s, 0, 1)
             push(s + 1, 1)
-            rest(functools.partial(proc_chunk, s), 2)
         else:
-            rest(functools.partial(proc_chunk, s), 0)
+            loop(0, 2, functools.partial(proc_chunk, s, 0))
+        loop(0, 2, functools.partial(proc_chunk, s, 1))
 
     def restore(b, _):
         mine[b] = state[place(b)]
@@ -488,10 +531,9 @@
     store = pltpu.make_async_copy(mine, out_h, local_sem.at[0])
     store.start()
     for p in range(PARTS):
-        for way in (0, 1):
-            relay_copy(p, way).wait_send()
-            for h in (0, 1):
-                gather_copy(p, way, h).wait_send()
+        if p >= 2:
+            spread_out(p)
+
         def sent(j):
             loop(1, 4, lambda by: mid_copy(p, by, j).wait_send())
             loop(1, 8, lambda k: last_copy(p, j, k).wait_send())
@@ -546,8 +588,8 @@
             *[vm(holding, BF16)] * 4,
             vm((blocks, rows, width), BF16),
             vm((blocks, rows, width), BF16),
-            vm((blocks + 2 * rim, rows, width), BF16),
-            vm((blocks + 2 * rim, rows, width), BF16),
+            vm((2 * rim, rows, width), BF16),
+            vm((2 * rim, rows, width), BF16),
             vm((rim, rows, width), BF16),
             vm((rim, rows, width), BF16),
             vm((1, peers), jnp.int32),

time: 140 us -> 140 us (level)
  no operation moved by 1% of the time
where the time goes in v5:
time: 140 us
  Pallas kernels  138 us (99%)
  local copies, waits for them, and re-layouts  2.26 us (2%)
    pallas_call x1, Pallas kernels, on_device(): pl.pallas_call(whole_kernel, out_shape=jax.ShapeDtypeStruct((blocks, rows...  138 us

profile of v5, /device:TPU:1, one launch (start us, length us, event | category | flops | bytes accessed | tf_op | source)
XLA Modules:
  0.0 140.0 jit_solution(9317108433019654481)
XLA Ops:
  0.0 137.7 %encoder_and_steps.1 = bf16[16,64,512]{2,1,0:T(8,128)(2,1)} custom-call(s32[1,224]{1,0:T(1,128)} %g_src_h.1, s32[1,224]{1,0:T(1,128)} %g_dst_h.1, s32[1,112]{1,0:T(1,128)} %m_src_h.1, s32[1,112]{1,0:T(1,128)} %m_dst_h.1, s32[1,8]{1,0:T(1,128)} %halo_h.1, s32[1,128]{1,0:T(1,128)} %send_row.1, bf16[32,64,512]{2,1,0:T(8,128)(2,1)} %bitcast.7, ...), custom_call_target="tpu_custom_call" | custom-call | tf_op jit(solution)/shard_map/encoder_and_steps/pallas_call | solution.py:565
  137.7 2.3 %copy.22 = bf16[1024,512]{1,0:T(8,128)(2,1)} copy(bf16[1024,512]{1,0:T(8,128)(2,1)} %bitcast.6) | data formatting | bytes 2097152

commit v6 on v5

--- a/solution.py
+++ b/solution.py
@@ -427,15 +427,15 @@
     n_dom = lax.axis_size("dom")
     upper, lower = moved("x", 1), moved("x", 3)
     quarter = blocks // 4
-    half_rim = rim // 2
+    pieces = ((0, 2), (2, 2), (4, rim - 4))
 
     def halo(s, h):
-        src = payload[s].at[pl.ds(h * half_rim, half_rim)]
+        src = payload[s].at[pl.ds(*pieces[h])]
         up = pltpu.make_async_remote_copy(
-            src, ptable[s].at[pl.ds(h * half_rim, half_rim)],
+            src, ptable[s].at[pl.ds(*pieces[h])],
             send_sem.at[s, 0, h], recv_sem.at[s, 0, h], device_id=upper, device_id_type=MESH)
         down = pltpu.make_async_remote_copy(
-            src, ptable[s].at[pl.ds(rim + h * half_rim, half_rim)],
+            src, ptable[s].at[pl.ds(rim + pieces[h][0], pieces[h][1])],
             send_sem.at[s, 1, h], recv_sem.at[s, 1, h], device_id=lower, device_id_type=MESH)
         return up, down
 
@@ -456,16 +456,14 @@
 
         loop(0, blocks, one)
 
-    def rim_part(s, h, k):
-        c = 2 * h + k
-        some = pl.ds(k * quarter * PARTS, quarter * PARTS)
-        acc = jnp.zeros((quarter * rows, width), F32)
+    def rim_part(s, h, k, n):
+        some = pl.ds(k * PARTS, n * PARTS)
+        acc = jnp.zeros((n * rows, width), F32)
         for q in (0, 1):
-            dense = ag[s][2 * q + h][some].reshape(quarter * rows, rim * rows)
+            dense = ag[s][2 * q + h][some].reshape(n * rows, rim * rows)
             acc = acc + mm(dense, ptable[s][pl.ds(q * rim, rim)].reshape(rim * rows, width))
-        at_c = c // 2, lax.rem(c, 2)
         for level in (0, 1):
-            acc = acc + table[(level, *at_c)].reshape(quarter * rows, width).astype(F32)
+            acc = acc + table[level, h, k // 4, pl.ds(lax.rem(k, 4), n)].reshape(n * rows, width).astype(F32)
         return acc.astype(BF16)
 
     def update(old, agg, w_in, w_out, gain):
@@ -477,51 +475,52 @@
         normed = cen * lax.rsqrt(var + 1e-05) * gain
         return (old.astype(F32) + normed).astype(BF16)
 
-    def message(s, c, new):
+    def message(s, first, n, new):
         h = silu(mm(new, m_in[s])).astype(BF16)
         msg = mm(h, m_out[s]).astype(BF16)
-        mine[pl.ds(c * quarter, quarter)] = msg.reshape(quarter, rows, width)
+        mine[pl.ds(first, n)] = msg.reshape(n, rows, width)
 
     def push(s, h):
-        for i in range(half_rim):
-            payload[s][h * half_rim + i] = mine[halo_at(h * half_rim + i)]
+        first, count = pieces[h]
+        for i in range(first, first + count):
+            payload[s][i] = mine[halo_at(i)]
         for c in halo(s, h):
             c.start()
 
-    def enc_chunk(c):
+    def enc_chunk(first, n):
         agg = jnp.concatenate([
-            tiles_sum(from_grid, g_src, wt_g, slots_g, c * quarter + i).astype(BF16) for i in range(quarter)], axis=0)
-        old = jnp.concatenate([latent[perm(c * quarter + i)] for i in range(quarter)], axis=0)
+            tiles_sum(from_grid, g_src, wt_g, slots_g, first + i).astype(BF16) for i in range(n)], axis=0)
+        old = jnp.concatenate([latent[perm(first + i)] for i in range(n)], axis=0)
         new = update(old, agg, e_in, e_out, e_gain[...])
-        state[pl.ds(c * quarter, quarter)] = new.reshape(quarter, rows, width)
-        message(0, c, new)
-
-    def proc_chunk(s, h, k):
-        c = 2 * h + k
-        old = state[pl.ds(c * quarter, quarter)].reshape(quarter * rows, width)
-        new = update(old, rim_part(s, h, k), u_in.at[s], u_out.at[s], u_gain[pl.ds(s, 1), :])
-        state[pl.ds(c * quarter, quarter)] = new.reshape(quarter, rows, width)
+        state[pl.ds(first, n)] = new.reshape(n, rows, width)
+        message(0, first, n, new)
+
+    def proc_chunk(s, h, k, n):
+        first = h * (blocks // 2) + k
+        old = state[pl.ds(first, n)].reshape(n * rows, width)
+        new = update(old, rim_part(s, h, k, n), u_in.at[s], u_out.at[s], u_gain[pl.ds(s, 1), :])
+        state[pl.ds(first, n)] = new.reshape(n, rows, width)
         if s + 1 < steps:
-            message(s + 1, c, new)
-
-    enc_chunk(0)
-    push(0, 0)
-    enc_chunk(1)
-    push(0, 1)
-    loop(2, 4, enc_chunk)
+            message(s + 1, first, n, new)
+
+    for h, (first, n) in enumerate(pieces):
+        enc_chunk(first, n)
+        push(0, h)
+    loop(2, 4, lambda c: enc_chunk(c * quarter, quarter))
     for s in range(steps):
         own_part(s)
-        for h in range(2):
+        for h in range(len(pieces)):
             for c in halo(s, h):
                 c.wait()
         if s + 1 < steps:
-            proc_chunk(s, 0, 0)
-            push(s + 1, 0)
-            proc_chunk(s, 0, 1)
-            push(s + 1, 1)
+            for h, (first, n) in enumerate(pieces):
+                proc_chunk(s, 0, first, n)
+                push(s + 1, h)
+            loop(0, 2, lambda c: proc_chunk(s, 1, c * quarter, quarter))
         else:
-            loop(0, 2, functools.partial(proc_chunk, s, 0))
-        loop(0, 2, functools.partial(proc_chunk, s, 1))
+            for h in (0, 1):
+                proc_chunk(s, h, 0, quarter)
+                proc_chunk(s, h, quarter, quarter)
 
     def restore(b, _):
         mine[b] = state[place(b)]
@@ -598,7 +597,7 @@
             dma((8,)), dma((19,)), dma((3, 3)), dma((3, 3)),
             dma((4, 2, 2)), dma((4, 2, 2)), dma((4, 2)), dma((4, 2)),
             dma((4, 3, 4)), dma((4, 3, 4)), dma((4, 4, 8)), dma((4, 4, 8)), dma((4, 4)), dma((8,)),
-            dma((steps, 2, 2)), dma((steps, 2, 2)),
+            dma((steps, 2, 3)), dma((steps, 2, 3)),
         ],
         compiler_params=pltpu.CompilerParams(
             collective_id=0, has_side_effects=True, vmem_limit_bytes=62 * 2**20

time: 140 us -> 138 us (0.986)
  Pallas kernels: 138 us -> 136 us
    pallas_call x1, Pallas kernels: 138 us -> 136 us  [on_device(): pl.pallas_call(whole_kernel, out_shape=jax.ShapeDtypeStruct((blocks, rows...]
where the time goes in v6:
time: 138 us
  Pallas kernels  136 us (99%)
  local copies, waits for them, and re-layouts  2.26 us (2%)
    pallas_call x1, Pallas kernels, on_device(): pl.pallas_call(whole_kernel, out_shape=jax.ShapeDtypeStruct((blocks, rows...  136 us

profile of v6, /device:TPU:1, one launch (start us, length us, event | category | flops | bytes accessed | tf_op | source)
XLA Modules:
  0.0 137.8 jit_solution(515458967623596619)
XLA Ops:
  0.0 135.5 %encoder_and_steps.1 = bf16[16,64,512]{2,1,0:T(8,128)(2,1)} custom-call(s32[1,224]{1,0:T(1,128)} %g_src_h.1, s32[1,224]{1,0:T(1,128)} %g_dst_h.1, s32[1,112]{1,0:T(1,128)} %m_src_h.1, s32[1,112]{1,0:T(1,128)} %m_dst_h.1, s32[1,8]{1,0:T(1,128)} %halo_h.1, s32[1,128]{1,0:T(1,128)} %send_row.1, bf16[32,64,512]{2,1,0:T(8,128)(2,1)} %bitcast.7, ...), custom_call_target="tpu_custom_call" | custom-call | tf_op jit(solution)/shard_map/encoder_and_steps/pallas_call | solution.py:564
  135.5 2.3 %copy.22 = bf16[1024,512]{1,0:T(8,128)(2,1)} copy(bf16[1024,512]{1,0:T(8,128)(2,1)} %bitcast.6) | data formatting | bytes 2097152
